TPU v7x, 128 devices: a whole 4x4x4 slice. The times are simulated.
128 devices in a mesh: dp: 32 (over z, x, core), db: 4 (over y).
Axes of the slice: x: 4, y: 4, z: 4, core: 2. Of those that a mesh axis runs over, the one named last changes fastest.
Arguments:
- queries: bfloat16 [18432, 4096], P('dp', 'db'), may hold values from -100 to 100
- cotangent: bfloat16 [18432, 4096], P('dp', 'db'), may hold values from -6 to 6
- db_states: bfloat16 [1024, 128, 896], P('dp', 'db'), may hold values from -6 to 6
- key_weight: bfloat16 [896, 4096], P(None, 'db'), may hold values from -0.1875 to 0.1875
- value_weight: bfloat16 [896, 4096], P(None, 'db'), may hold values from -0.1875 to 0.1875
- conv_kernel: float32 [3, 896], replicated, may hold values from -2.5 to 2.5
- nbr_owner: int32 [288, 2], P('dp'), may hold values from 0 to 31, all different within a row; in each aligned block of 9 rows (0 to 8, 9 to 17, ...) at most 2 rows name the same one
- nbr_row: int32 [288, 2], P('dp'), may hold values from 0 to 31
Outputs:
- attended: bfloat16 [18432, 4096], P('dp', 'db')
- grad_queries: bfloat16 [18432, 4096], P('dp', 'db')
- grad_states: float32 [1024, 128, 896], P('dp', 'db')
- grad_key_weight: float32 [896, 4096], P(None, 'db')
- grad_value_weight: float32 [896, 4096], P(None, 'db')
- grad_kernel: float32 [3, 896], replicated
Inputs may be any that keep to these rules, and one draw needn't show every extreme that they name: `nbr_owner`: in the 9 spans of one index of dp no owner is named more than 2 times, a bound that some block reaches; the 2 neighbours of a span have different owners.
All inputs are finite; a program needn't handle non-finite values.
Results may differ from a plain program's by a relative error of at most 0.035.
The roundings to bfloat16 on the way count: a program that leaves them out, or rounds other values in their place, can miss the bound.
Values may be sent and summed in bfloat16 or wider, within the bound.
A program may use at most 192 MiB of HBM per device.

v0:
```python
import math

import jax
import jax.numpy as jnp
from jax import lax
from jax.sharding import PartitionSpec as P

HD = 128
ENC = 896
SPAN = 64
NBR = 2
NLEN = 128
KW = 3


def extended(block, sides, width):
    for axis, dim in sides:
        count = lax.axis_size(axis)
        forward = [(i, i + 1) for i in range(count - 1)]
        backward = [(target, source) for source, target in forward]
        low = lax.ppermute(
            lax.slice_in_dim(block, block.shape[dim] - width, None, axis=dim), axis, forward
        )
        high = lax.ppermute(lax.slice_in_dim(block, 0, width, axis=dim), axis, backward)
        block = jnp.concatenate([low, block, high], axis=dim)
    return block


def conv_apply(padded, kernel, length):
    summed = kernel[0] * padded[:, 0:length, :].astype(jnp.float32)
    for offset in range(1, KW):
        summed = summed + kernel[offset] * padded[:, offset : offset + length, :].astype(
            jnp.float32
        )
    return summed


def conv_adjoint(grad_padded, kernel, length):
    final_tap = KW - 1
    summed = kernel[0] * grad_padded[:, final_tap : final_tap + length, :]
    for offset in range(1, KW):
        begin = final_tap - offset
        summed = summed + kernel[offset] * grad_padded[:, begin : begin + length, :]
    return summed


def taps_gradient(grad_mixed, padded, length):
    return jnp.stack(
        [
            jnp.sum(
                grad_mixed * padded[:, offset : offset + length, :].astype(jnp.float32), axis=(0, 1)
            )
            for offset in range(KW)
        ]
    )


def shards(
    queries, cotangent, db_states, key_weight, value_weight, conv_kernel, nbr_owner, nbr_row
):
    half_taps = (KW - 1) // 2
    score_scale = 1.0 / math.sqrt(HD)
    owners = lax.axis_size("dp")
    span_count = nbr_owner.shape[0]
    request_count = span_count * NBR
    capacity = max(2, (request_count + owners - 1) // owners)
    quarter = db_states.shape[1]
    local_blocks = db_states.shape[0]
    slots_total = owners * capacity
    local_width = key_weight.shape[1]
    local_heads = local_width // HD
    owner_flat = nbr_owner.reshape(request_count)
    row_flat = nbr_row.reshape(request_count)
    positions = jnp.arange(request_count, dtype=jnp.int32)
    same_owner = owner_flat[:, None] == owner_flat[None, :]
    earlier = positions[:, None] > positions[None, :]
    slot_index = jnp.sum(jnp.logical_and(same_owner, earlier).astype(jnp.int32), axis=1)
    target = owner_flat * capacity + slot_index
    slot_hits = target[:, None] == jnp.arange(slots_total, dtype=jnp.int32)[None, :]
    used_slot = jnp.any(slot_hits, axis=0)
    row_sent = jnp.sum(jnp.where(slot_hits, row_flat[:, None], 0), axis=0)
    row_table = jnp.where(used_slot, row_sent, -1).reshape(owners, capacity)
    slot_matrix = slot_hits.astype(jnp.bfloat16)
    states_flat = db_states.reshape(local_blocks, quarter * ENC)
    asked = lax.all_to_all(row_table, "dp", split_axis=0, concat_axis=0, tiled=True)
    sources = asked.shape[0]
    items = asked.shape[1]
    asked_flat = asked.reshape(sources * items)
    picker = (asked_flat[:, None] == jnp.arange(local_blocks, dtype=jnp.int32)[None, :]).astype(
        jnp.bfloat16
    )
    fetched = jnp.dot(picker, states_flat, preferred_element_type=jnp.float32).astype(jnp.bfloat16)
    fetched = fetched.reshape(sources, items, quarter, ENC)
    replied = lax.all_to_all(fetched, "dp", split_axis=0, concat_axis=0, tiled=True)
    received = jnp.dot(
        slot_matrix, replied.reshape(slots_total, quarter * ENC), preferred_element_type=jnp.float32
    )
    received = received.astype(jnp.bfloat16).reshape(request_count, quarter, ENC)
    padded_part = extended(received, (("db", 1),), half_taps)
    mixed_part = conv_apply(padded_part, conv_kernel, quarter).astype(jnp.bfloat16)
    mixed = lax.all_gather(mixed_part, "db", axis=1, tiled=True)
    mixed_flat = mixed.reshape(request_count * NLEN, ENC)
    keys = jnp.dot(mixed_flat, key_weight, preferred_element_type=jnp.float32).astype(jnp.bfloat16)
    values = jnp.dot(mixed_flat, value_weight, preferred_element_type=jnp.float32).astype(
        jnp.bfloat16
    )
    key_heads = keys.reshape(span_count, NBR * NLEN, local_heads, HD)
    value_heads = values.reshape(span_count, NBR * NLEN, local_heads, HD)
    query_heads = queries.reshape(span_count, SPAN, local_heads, HD)
    grad_heads = cotangent.reshape(span_count, SPAN, local_heads, HD)
    scores = (
        jnp.einsum("cqhd,ckhd->chqk", query_heads, key_heads, preferred_element_type=jnp.float32)
        * score_scale
    )
    highest = jnp.max(scores, axis=-1, keepdims=True)
    expo = jnp.exp(scores - highest)
    probs = expo / jnp.sum(expo, axis=-1, keepdims=True)
    probs_b = probs.astype(jnp.bfloat16)
    attended = jnp.einsum(
        "chqk,ckhd->cqhd", probs_b, value_heads, preferred_element_type=jnp.float32
    ).astype(jnp.bfloat16)
    grad_probs = jnp.einsum(
        "cqhd,ckhd->chqk", grad_heads, value_heads, preferred_element_type=jnp.float32
    )
    grad_values = jnp.einsum(
        "chqk,cqhd->ckhd", probs_b, grad_heads, preferred_element_type=jnp.float32
    ).astype(jnp.bfloat16)
    inner = jnp.sum(grad_probs * probs, axis=-1, keepdims=True)
    grad_scores = (score_scale * probs * (grad_probs - inner)).astype(jnp.bfloat16)
    grad_query = jnp.einsum(
        "chqk,ckhd->cqhd", grad_scores, key_heads, preferred_element_type=jnp.float32
    ).astype(jnp.bfloat16)
    grad_keys = jnp.einsum(
        "chqk,cqhd->ckhd", grad_scores, query_heads, preferred_element_type=jnp.float32
    ).astype(jnp.bfloat16)
    keys_flat = grad_keys.reshape(request_count * NLEN, local_width)
    values_flat = grad_values.reshape(request_count * NLEN, local_width)
    key_term = jnp.einsum("ne,nf->ef", mixed_flat, keys_flat, preferred_element_type=jnp.float32)
    value_term = jnp.einsum(
        "ne,nf->ef", mixed_flat, values_flat, preferred_element_type=jnp.float32
    )
    grad_mixed = jnp.einsum("nf,ef->ne", keys_flat, key_weight, preferred_element_type=jnp.float32)
    grad_mixed = grad_mixed + jnp.einsum(
        "nf,ef->ne", values_flat, value_weight, preferred_element_type=jnp.float32
    )
    grad_mixed = grad_mixed.reshape(request_count, NLEN, ENC)
    grad_mixed_part = lax.psum_scatter(grad_mixed, "db", scatter_dimension=1, tiled=True)
    grad_padded = extended(grad_mixed_part, (("db", 1),), half_taps)
    grad_raw = conv_adjoint(grad_padded, conv_kernel, quarter)
    taps_term = taps_gradient(grad_mixed_part, padded_part, quarter)
    grad_raw_b = grad_raw.astype(jnp.bfloat16).reshape(request_count, quarter * ENC)
    grad_send = jnp.einsum(
        "ns,nf->sf", slot_matrix, grad_raw_b, preferred_element_type=jnp.float32
    ).astype(jnp.bfloat16)
    grad_send = grad_send.reshape(owners, capacity, quarter, ENC)
    grad_back = lax.all_to_all(grad_send, "dp", split_axis=0, concat_axis=0, tiled=True)
    asked_flat = asked.reshape(slots_total)
    picker_back = (
        jnp.arange(local_blocks, dtype=jnp.int32)[:, None] == asked_flat[None, :]
    ).astype(jnp.bfloat16)
    grad_states = jnp.dot(
        picker_back,
        grad_back.reshape(slots_total, quarter * ENC),
        preferred_element_type=jnp.float32,
    )
    grad_states = grad_states.reshape(local_blocks, quarter, ENC)
    grad_key_weight, grad_value_weight = lax.psum((key_term, value_term), "dp")
    grad_kernel = lax.psum(taps_term, ("dp", "db"))
    return (
        attended.reshape(span_count * SPAN, local_width),
        grad_query.reshape(span_count * SPAN, local_width),
        grad_states,
        grad_key_weight,
        grad_value_weight,
        grad_kernel,
    )


def solution(mesh):
    return jax.shard_map(
        shards,
        mesh=mesh,
        in_specs=(
            P("dp", "db"),
            P("dp", "db"),
            P("dp", "db", None),
            P(None, "db"),
            P(None, "db"),
            P(),
            P("dp", None),
            P("dp", None),
        ),
        out_specs=(
            P("dp", "db"),
            P("dp", "db"),
            P("dp", "db", None),
            P(None, "db"),
            P(None, "db"),
            P(),
        ),
        check_vma=False,
    )
```

profile of v0, /device:TPU:1, one launch (start us, length us, event | category | flops | bytes accessed | tf_op | source)
XLA Modules:
  0.0 488.1 jit_solution(10462257573725515154)
XLA Ops:
  10.1 9.4 %all-to-all-start = ((s32[32,1,2]{2,1,0:T(1,128)}), s32[32,1,2]{2,1,0:T(1,128)S(1)}, u32[]{:S(2)}, u32[]{:S(2)}) async-start(s32[32,1,2]{2,1,0:T(1,128)} %bitcast), calls=%async_computation | async-start | bytes 32768 | tf_op jit(solution)/shard_map/all_to_all | solution.py:85
  19.6 3.3 copy.76
  22.9 3.5 all-to-all-done
  27.7 2.7 convolution_convert_fusion.1
  31.0 49.0 %all_to_all.16 = bf16[32,2,32,896]{3,2,1,0:T(8,128)(2,1)S(1)} all-to-all(bf16[32,2,32,896]{3,2,1,0:T(8,128)(2,1)S(1)} %bitcast.131), channel_id=1, replica_groups=mesh['dp'=32,'db'=4] {'dp'}, dimensions={0} | all-to-all | bytes 7340032 | tf_op jit(solution)/shard_map/all_to_all | solution.py:94
  82.3 3.2 collective-permute-start
  87.0 3.5 collective-permute-done.1
  94.6 2.6 copy.84
  97.2 41.8 %all-gather.2.cloned.1.call-done = bf16[18,128,896]{2,1,0:T(8,128)(2,1)} async-done(((bf16[18,32,896]{2,1,0:T(8,128)(2,1)}), bf16[18,128,896]{2,1,0:T(8,128)(2,1)}) %all-gather.2.cloned.1.call-update) | async-done | bytes 4128784 | tf_op jit(solution)/shard_map/all_gather | solution.py:101
  139.0 7.4 %fusion.33 = bf16[288,8,8,128]{3,1,2,0:T(8,128)(2,1)S(1)} fusion(bf16[2304,896]{1,0:T(8,128)(2,1)} %bitcast.159, bf16[896,1024]{1,0:T(8,128)(2,1)S(1)} %copy-done), kind=kOutput, calls=%fused_computation.50 | convolution fusion | flops 4230217728 | bytes 10682368 | tf_op jit(solution)/shard_map/dot_general | solution.py:103
  149.2 5.4 %fusion.32 = bf16[288,8,8,128]{3,1,2,0:T(8,128)(2,1)S(1)} fusion(bf16[2304,896]{1,0:T(8,128)(2,1)S(1)} %bitcast.162, bf16[896,1024]{1,0:T(8,128)(2,1)S(1)} %copy-done.17), kind=kOutput, calls=%fused_computation.49 | convolution fusion | flops 4230217728 | bytes 10682368 | tf_op jit(solution)/shard_map/dot_general | solution.py:104
  154.6 3.4 copy.82
  159.8 3.6 fusion.82
  163.3 15.7 %convert_bitcast_fusion = bf16[9,256,8,128]{3,1,2,0:T(8,128)(2,1)} fusion(bf16[9,64,8,128]{3,2,1,0:T(8,128)(2,1)} %bitcast.157, f32[9,8,64]{2,1,0:T(8,128)S(1)} %get-tuple-element.43, f32[9,8,256,64]{2,3,1,0:T(8,128)} %copy-done.5), kind=kOutput, calls=%fused_computation.23 | convolution fusion | flops 310252288 | bytes 10635264 | tf_op jit(solution)/shard_map/chqk,cqhd->ckhd/dot_general | solution.py:125
  179.0 5.7 %copy.72 = bf16[9,256,8,128]{3,2,1,0:T(8,128)(2,1)S(1)} copy(bf16[9,256,8,128]{3,1,2,0:T(8,128)(2,1)} %convert_bitcast_fusion) | data formatting | bytes 9437184 | tf_op jit(solution)/shard_map/convert_element_type | solution.py:127
  184.8 5.8 %fusion.8 = (f32[9,8,64]{2,1,0:T(8,128)S(1)}, f32[9,8,256,64]{2,3,1,0:T(8,128)S(1)}) fusion(f32[9,8,64,256]{3,2,1,0:T(8,128)S(1)} %copy-done.4, f32[9,8,64]{2,1,0:T(8,128)S(1)} %get-tuple-element.43, bf16[9,64,8,128]{3,2,1,0:T(8,128)(2,1)S(1)} %bitcast.158, bf16[9,256,8,128]{3,2,1,0:T(8,128)(2,1)} %bitcast.146), kind=kOutput, calls=%fused_computation.16 | convolution fusion | flops 305524224 | bytes 15372288 | tf_op jit(solution)/shard_map/cqhd,ckhd->chqk/dot_general | solution.py:122
  195.2 3.3 copy.70
  198.5 7.3 %fusion.6 = f32[2304,896]{1,0:T(8,128)} fusion(bf16[896,1024]{1,0:T(8,128)(2,1)S(1)} %copy-done, bf16[288,8,8,128]{3,2,1,0:T(8,128)(2,1)S(1)} %bitcast.150), kind=kOutput, calls=%fused_computation.12 | convolution fusion | flops 4227858432 | bytes 14811136 | tf_op jit(solution)/shard_map/nf,ef->ne/dot_general | solution.py:142
  205.7 9.5 %convolution_add_fusion = f32[2304,896]{1,0:T(8,128)} fusion(f32[2304,896]{1,0:T(8,128)} %fusion.6, bf16[896,1024]{1,0:T(8,128)(2,1)S(1)} %copy-done.18, bf16[288,8,8,128]{3,2,1,0:T(8,128)(2,1)S(1)} %bitcast.148), kind=kOutput, calls=%fused_computation.4 | convolution fusion | flops 4229922816 | bytes 23068672 | tf_op jit(solution)/shard_map/nf,ef->ne/dot_general | solution.py:143
  215.2 80.0 %reduce-scatter.2.cloned.1.call-done = f32[18,32,896]{2,1,0:T(8,128)} async-done(((f32[18,128,896]{2,1,0:T(8,128)}), f32[18,32,896]{2,1,0:T(8,128)}) %reduce-scatter.2.cloned.1.call-update) | async-done | bytes 2064400 | tf_op jit(solution)/shard_map/reduce_scatter | solution.py:147
  297.9 4.7 collective-permute-start.3
  302.5 9.9 %fusion.4 = f32[896,1024]{1,0:T(8,128)} fusion(bf16[2304,896]{1,0:T(8,128)(2,1)} %bitcast.160, bf16[288,8,8,128]{3,2,1,0:T(8,128)(2,1)} %bitcast.151), kind=kOutput, calls=%fused_computation.10 | convolution fusion | flops 4227858432 | bytes 12517376 | tf_op jit(solution)/shard_map/ne,nf->ef/dot_general | solution.py:138
  316.5 2.4 copy.89
  318.9 8.2 %all-to-all-start.2 = ((bf16[32,2,32,896]{3,2,1,0:T(8,128)(2,1)}), bf16[32,2,32,896]{3,2,1,0:T(8,128)(2,1)}, u32[]{:S(2)}, u32[]{:S(2)}) async-start(bf16[32,2,32,896]{3,2,1,0:T(8,128)(2,1)} %bitcast.130), calls=%async_computation.3 | async-start | bytes 7340032 | tf_op jit(solution)/shard_map/all_to_all | solution.py:156
  327.4 9.9 %fusion.1 = f32[896,1024]{1,0:T(8,128)} fusion(bf16[2304,896]{1,0:T(8,128)(2,1)} %bitcast.161, bf16[288,8,8,128]{3,2,1,0:T(8,128)(2,1)} %bitcast.149), kind=kOutput, calls=%fused_computation.7 | convolution fusion | flops 4227858432 | bytes 12517376 | tf_op jit(solution)/shard_map/ne,nf->ef/dot_general | solution.py:139
  337.2 3.8 fusion.54
  341.9 14.0 %fusion.51 = bf16[9,64,8,128]{3,1,2,0:T(8,128)(2,1)S(1)} fusion(bf16[9,256,8,128]{3,2,1,0:T(8,128)(2,1)} %bitcast.147, f32[9,8,64]{2,1,0:T(8,128)S(1)} %get-tuple-element.43, f32[9,8,256,64]{2,3,1,0:T(8,128)} %copy-done.5), kind=kOutput, calls=%fused_computation.66 | convolution fusion | flops 308482816 | bytes 10635264 | tf_op jit(solution)/shard_map/chqk,ckhd->cqhd/dot_general | solution.py:119
  359.0 74.7 %psum.23 = f32[3,896]{1,0:T(4,128)} all-reduce(f32[3,896]{1,0:T(4,128)S(1)} %pad_maximum_fusion.4), channel_id=1, replica_groups=mesh['dp'=32,'db'=4] {'dp','db'}, use_global_device_ids=true, to_apply=%region_12.13 | all-reduce | flops 2688 | bytes 21504 | tf_op jit(solution)/shard_map/psum | solution.py:168
  433.7 4.3 fusion.26
  438.1 4.0 copy.74
  442.0 32.9 %all-reduce.3.cloned.1.call-done = (f32[896,1024]{1,0:T(8,128)}, f32[896,1024]{1,0:T(8,128)}) async-done(((f32[896,1024]{1,0:T(8,128)}, f32[896,1024]{1,0:T(8,128)}), (f32[896,1024]{1,0:T(8,128)}, f32[896,1024]{1,0:T(8,128)})) %all-reduce.3.cloned.1.call-update) | async-done | bytes 7340048 | tf_op jit(solution)/shard_map/psum | solution.py:167
  474.9 4.5 copy.146
  (89 shorter events, 34.3 us)
Async XLA Ops:
  7.2 131.8 %copy-start = (bf16[896,1024]{1,0:T(8,128)(2,1)S(1)}, bf16[896,1024]{1,0:T(8,128)(2,1)}, u32[]{:S(2)}) copy-start(bf16[896,1024]{1,0:T(8,128)(2,1)} %param.11) | copy-start | bytes 5505028
  10.1 16.3 %all-to-all-start = ((s32[32,1,2]{2,1,0:T(1,128)}), s32[32,1,2]{2,1,0:T(1,128)S(1)}, u32[]{:S(2)}, u32[]{:S(2)}) async-start(s32[32,1,2]{2,1,0:T(1,128)} %bitcast), calls=%async_computation | async-start | bytes 32768 | tf_op jit(solution)/shard_map/all_to_all | solution.py:85
  19.6 119.4 %all-gather.2.cloned.1.call-start = ((), (), s32[]{:S(2)}) async-start(), calls=%async_computation.4 | async-start | bytes 5160960 | tf_op jit(solution)/shard_map/all_gather | solution.py:101
  81.4 5.5 %copy-start.15 = (f32[3,896]{1,0:T(4,128)S(1)}, f32[3,896]{1,0:T(4,128)}, u32[]{:S(2)}) copy-start(f32[3,896]{1,0:T(4,128)} %param.13) | copy-start | bytes 32260
  82.2 4.7 copy-start.8
  82.3 4.7 collective-permute-start
  85.6 5.0 %collective-permute-start.1 = (bf16[18,1,896]{2,1,0:T(2,128)(2,1)S(1)}, bf16[18,1,896]{2,1,0:T(2,128)(2,1)S(1)}, u32[]{:S(2)}, u32[]{:S(2)}) collective-permute-start(bf16[18,1,896]{2,1,0:T(2,128)(2,1)S(1)} %get-tuple-element.42), channel_id=1, source_target_pairs={{1,0},{2,1},{3,2},{5,4},{6,5},{7,6},{9,8},{10,9},{11,10},{13,12},{... | collective-permute-start | bytes 96776 | tf_op jit(solution)/shard_map/ppermute | solution.py:24
  87.0 3.5 copy-start.6
  92.4 202.8 %reduce-scatter.2.cloned.1.call-start = ((), (), s32[]{:S(2)}) async-start(), calls=%async_computation.5 | async-start | bytes 10321920 | tf_op jit(solution)/shard_map/reduce_scatter | solution.py:147
  146.4 2.2 copy-start.16
  146.4 2.7 copy-start.17
  149.2 8.8 %copy-start.2 = (bf16[288,8,8,128]{3,2,1,0:T(8,128)(2,1)}, bf16[288,8,8,128]{3,2,1,0:T(8,128)(2,1)S(1)}, u32[]{:S(2)}) copy-start(bf16[288,8,8,128]{3,2,1,0:T(8,128)(2,1)S(1)} %copy.80) | copy-start | bytes 14155780
  159.7 3.6 copy-start.5
  179.0 5.8 %copy-start.4 = (f32[9,8,64,256]{3,2,1,0:T(8,128)S(1)}, f32[9,8,64,256]{3,2,1,0:T(8,128)}, u32[]{:S(2)}) copy-start(f32[9,8,64,256]{3,2,1,0:T(8,128)} %get-tuple-element.44) | copy-start | bytes 14155780
  179.0 5.8 %copy-start.14 = (bf16[72,8,8,128]{3,2,1,0:T(8,128)(2,1)S(1)}, bf16[72,8,8,128]{3,2,1,0:T(8,128)(2,1)}, u32[]{:S(2)}) copy-start(bf16[72,8,8,128]{3,2,1,0:T(8,128)(2,1)} %copy.84) | copy-start | bytes 3538948
  184.7 21.0 %copy-start.10 = (bf16[9,256,8,128]{3,2,1,0:T(8,128)(2,1)}, bf16[9,256,8,128]{3,2,1,0:T(8,128)(2,1)S(1)}, u32[]{:S(2)}) copy-start(bf16[9,256,8,128]{3,2,1,0:T(8,128)(2,1)S(1)} %copy.72) | copy-start | bytes 14155780
  192.1 1.4 copy-start.3
  198.4 7.3 %copy-start.11 = (bf16[9,256,8,128]{3,2,1,0:T(8,128)(2,1)}, bf16[9,256,8,128]{3,2,1,0:T(8,128)(2,1)S(1)}, u32[]{:S(2)}) copy-start(bf16[9,256,8,128]{3,2,1,0:T(8,128)(2,1)S(1)} %copy.70) | copy-start | bytes 14155780
  198.4 7.3 %copy-start.18 = (bf16[896,1024]{1,0:T(8,128)(2,1)S(1)}, bf16[896,1024]{1,0:T(8,128)(2,1)}, u32[]{:S(2)}) copy-start(bf16[896,1024]{1,0:T(8,128)(2,1)} %param.12) | copy-start | bytes 5505028
  296.5 15.9 %collective-permute-start.2 = (f32[18,1,896]{2,1,0:T(1,128)S(1)}, f32[18,1,896]{2,1,0:T(1,128)S(1)}, u32[]{:S(2)}, u32[]{:S(2)}) collective-permute-start(f32[18,1,896]{2,1,0:T(1,128)S(1)} %get-tuple-element.39), channel_id=1, source_target_pairs={{1,0},{2,1},{3,2},{5,4},{6,5},{7,6},{9,8},{10,9},{11,10},{13,12},{... | collective-permute-start | bytes 193544 | tf_op jit(solution)/shard_map/ppermute | solution.py:24
  297.8 14.6 %copy-start.7 = (bf16[18,32,896]{2,1,0:T(8,128)(2,1)S(1)}, bf16[18,32,896]{2,1,0:T(8,128)(2,1)}, u32[]{:S(2)}) copy-start(bf16[18,32,896]{2,1,0:T(8,128)(2,1)} %copy-done.6) | copy-start | bytes 3096580
  297.8 14.6 %copy-start.9 = (bf16[3,8,32,896]{3,2,1,0:T(8,128)(2,1)S(1)}, bf16[3,8,32,896]{3,2,1,0:T(8,128)(2,1)}, u32[]{:S(2)}) copy-start(bf16[3,8,32,896]{3,2,1,0:T(8,128)(2,1)} %copy-done.8) | copy-start | bytes 4128772
  297.8 14.6 %copy-start.13 = (f32[18,32,896]{2,1,0:T(8,128)S(1)}, f32[18,32,896]{2,1,0:T(8,128)}, u32[]{:S(2)}) copy-start(f32[18,32,896]{2,1,0:T(8,128)} %reduce-scatter.2.cloned.1.call-done) | copy-start | bytes 6193156
  297.9 14.6 %collective-permute-start.3 = (f32[18,1,896]{2,1,0:T(1,128)S(1)}, f32[18,1,896]{2,1,0:T(1,128)S(1)}, u32[]{:S(2)}, u32[]{:S(2)}) collective-permute-start(f32[18,1,896]{2,1,0:T(1,128)S(1)} %get-tuple-element.40), channel_id=1, source_target_pairs={{0,1},{1,2},{2,3},{4,5},{5,6},{6,7},{8,9},{9,10},{10,11},{12,13},{... | collective-permute-start | bytes 193544 | tf_op jit(solution)/shard_map/ppermute | solution.py:21
  318.9 114.8 %all-to-all-start.2 = ((bf16[32,2,32,896]{3,2,1,0:T(8,128)(2,1)}), bf16[32,2,32,896]{3,2,1,0:T(8,128)(2,1)}, u32[]{:S(2)}, u32[]{:S(2)}) async-start(bf16[32,2,32,896]{3,2,1,0:T(8,128)(2,1)} %bitcast.130), calls=%async_computation.3 | async-start | bytes 7340032 | tf_op jit(solution)/shard_map/all_to_all | solution.py:156
  327.1 147.8 %all-reduce.3.cloned.1.call-start = ((), (), s32[]{:S(2)}) async-start(), calls=%async_computation.6 | async-start | bytes 14680064 | tf_op jit(solution)/shard_map/psum | solution.py:167
  474.9 4.5 copy-start.12
  474.9 6.4 %copy-start.1 = (bf16[896,1024]{1,0:T(8,128)(2,1)S(1)}, bf16[896,1024]{1,0:T(8,128)(2,1)}, u32[]{:S(2)}) copy-start(bf16[896,1024]{1,0:T(8,128)(2,1)} %param.11) | copy-start | bytes 5505028
Sparse Core Ops, SparseCore 0:
  92.5 46.4 all-gather.1
  215.3 79.8 reduce-scatter.1
  337.4 137.5 all-reduce.2
where the time goes:
time: 494 us; the launch traced here: 488 us
  waiting for transfers between devices  162 us (33%)
  blocking collectives  124 us (25%)
  matrix products  101 us (20%)
  local copies, waits for them, and re-layouts  48.1 us (10%)
  starting transfers between devices  28.9 us (6%)
  between operations  14.4 us (3%)
  other arithmetic  10.2 us (2%)
    reduce_scatter x1, waiting for transfers between devices, shards(): lax.psum_scatter(grad_mixed, 'db', scatter_dimension=1, tiled=True)  80 us
    psum x1, blocking collectives, shards(): grad_kernel = lax.psum(taps_term, ('dp', 'db'))  74.7 us
    all_to_all x1, blocking collectives, shards(): lax.all_to_all(fetched, 'dp', split_axis=0, concat_axis=0, tiled=True)  49 us
    all_gather x1, waiting for transfers between devices, shards(): mixed = lax.all_gather(mixed_part, 'db', axis=1, tiled=True)  41.8 us
    psum x1, waiting for transfers between devices, shards(): grad_key_weight, grad_value_weight = lax.psum((key_term, value_term), 'dp')  32.9 us
    unnamed x54, local copies, waits for them, and re-layouts  32.2 us
    dot_general x1, matrix products, shards(): jnp.einsum('chqk,cqhd->ckhd', probs_b, grad_heads, preferred_element_type...  15.7 us
    dot_general x1, matrix products, shards(): jnp.einsum('chqk,ckhd->cqhd', probs_b, value_heads, preferred_element_typ...  14 us
  transfers between devices with their start and end apart: 9, of which 5 were waited for; matrix products, arithmetic and copies ran while one was open for 12% of the time, Pallas kernels for 0%

commit v1 on v0

v1 whole, which is shorter than its diff:
```python
import functools
import math

import jax
import jax.numpy as jnp
from jax import lax
from jax.experimental import pallas as pl
from jax.experimental.pallas import tpu as pltpu
from jax.sharding import PartitionSpec as P

HD = 128
ENC = 896
SPAN = 64
NBR = 2
NLEN = 128
KW = 3
LANES = 128
CHUNKS = ENC // LANES
F32 = jnp.float32
BF16 = jnp.bfloat16
NT = (((1,), (1,)), ((), ()))


def shifted(block):
    rows = block.shape[0]
    at = lax.broadcasted_iota(jnp.int32, block.shape, 0)
    down = jnp.where(at == 0, 0.0, pltpu.roll(block, 1, 0))
    up = jnp.where(at == rows - 1, 0.0, pltpu.roll(block, rows - 1, 0))
    return down, up


def core_kernel(
    heads,
    q_ref,
    g_ref,
    raw_ref,
    kw_ref,
    vw_ref,
    taps_ref,
    att_ref,
    gq_ref,
    part_ref,
    gkw_ref,
    gvw_ref,
    gt_ref,
    weights,
    mixed_s,
    mixed_t,
    grads,
    gm_s,
    taps_acc,
):
    span = pl.program_id(0)
    scale = 1.0 / math.sqrt(HD)
    keys_here = NBR * NLEN

    @pl.when(span == 0)
    def _():
        for h in range(heads):
            weights[:, 2 * h * HD : (2 * h + 1) * HD] = kw_ref[:, h * HD : (h + 1) * HD]
            weights[:, (2 * h + 1) * HD : (2 * h + 2) * HD] = vw_ref[:, h * HD : (h + 1) * HD]
        taps_acc[...] = jnp.zeros_like(taps_acc)

    for c in range(CHUNKS):
        cols = slice(c * LANES, (c + 1) * LANES)
        for n in range(NBR):
            raw = raw_ref[n, :, cols].astype(F32)
            down, up = shifted(raw)
            mixed = taps_ref[0:1, cols] * down
            mixed = mixed + taps_ref[1:2, cols] * raw
            mixed = mixed + taps_ref[2:3, cols] * up
            mixed_s[n * NLEN : (n + 1) * NLEN, cols] = mixed.astype(BF16)
    mixed = mixed_s[...]
    rows = pl.ds(pl.multiple_of(span * keys_here, keys_here), keys_here)
    mixed_t[:, rows] = mixed.T

    zeros = jnp.zeros((SPAN, HD), BF16)
    for h in range(heads):
        wide = slice(2 * h * HD, (2 * h + 2) * HD)
        cols = slice(h * HD, (h + 1) * HD)
        kv = jnp.dot(mixed, weights[:, wide], preferred_element_type=F32).astype(BF16)
        q = q_ref[:, cols]
        g = g_ref[:, cols]
        block_diag = jnp.concatenate(
            [jnp.concatenate([q, zeros], axis=1), jnp.concatenate([zeros, g], axis=1)], axis=0
        )
        both = lax.dot_general(block_diag, kv, NT, preferred_element_type=F32)
        scores = both[:SPAN] * scale
        grad_probs = both[SPAN:]
        expo = jnp.exp(scores - jnp.max(scores, axis=-1, keepdims=True))
        probs = expo / jnp.sum(expo, axis=-1, keepdims=True)
        inner = jnp.sum(grad_probs * probs, axis=-1, keepdims=True)
        grad_scores = scale * probs * (grad_probs - inner)
        stacked = jnp.concatenate([grad_scores, probs], axis=0).astype(BF16)
        out = jnp.dot(stacked, kv, preferred_element_type=F32)
        gq_ref[:, cols] = out[:SPAN, :HD].astype(BF16)
        att_ref[:, cols] = out[SPAN:, HD:].astype(BF16)
        grads[rows, wide] = jnp.dot(
            stacked.T, block_diag, preferred_element_type=F32
        ).astype(BF16)

    gm_s[...] = lax.dot_general(grads[rows, :], weights[...], NT, preferred_element_type=F32)
    for c in range(CHUNKS):
        cols = slice(c * LANES, (c + 1) * LANES)
        for n in range(NBR):
            gm = gm_s[n * NLEN : (n + 1) * NLEN, cols]
            gm_down, gm_up = shifted(gm)
            back = taps_ref[0:1, cols] * gm_up
            back = back + taps_ref[1:2, cols] * gm
            back = back + taps_ref[2:3, cols] * gm_down
            part_ref[n, :, cols] = back.astype(BF16)
            raw = raw_ref[n, :, cols].astype(F32)
            down, up = shifted(raw)
            for w, other in enumerate((down, raw, up)):
                taps_acc[w, :, cols] += jnp.sum(
                    (gm * other).reshape(NLEN // 8, 8, LANES), axis=0
                )

    @pl.when(span == pl.num_programs(0) - 1)
    def _():
        gt_ref[...] = jnp.sum(taps_acc[...], axis=1)

        def one_head(h, carry):
            wide = pl.ds(pl.multiple_of(h * 2 * HD, 2 * HD), 2 * HD)
            cols = pl.ds(pl.multiple_of(h * HD, HD), HD)
            term = jnp.dot(mixed_t[...], grads[:, wide], preferred_element_type=F32)
            gkw_ref[:, cols] = term[:, :HD].astype(BF16)
            gvw_ref[:, cols] = term[:, HD:].astype(BF16)
            return carry

        lax.fori_loop(0, heads, one_head, 0)


def core(queries, cotangent, raw, key_weight, value_weight, conv_kernel):
    tokens, width = queries.shape
    heads = width // HD
    spans = tokens // SPAN
    keys_all = spans * NBR * NLEN
    whole = lambda shape: pl.BlockSpec(
        shape, lambda i: (0,) * len(shape), pipeline_mode=pl.Buffered(1)
    )
    span_rows = pl.BlockSpec((SPAN, width), lambda i: (i, 0))
    blocks = pl.BlockSpec((NBR, NLEN, ENC), lambda i: (i, 0, 0))
    return pl.pallas_call(
        functools.partial(core_kernel, heads),
        grid=(spans,),
        in_specs=[
            span_rows,
            span_rows,
            blocks,
            whole((ENC, width)),
            whole((ENC, width)),
            whole((KW, ENC)),
        ],
        out_specs=[
            span_rows,
            span_rows,
            blocks,
            whole((ENC, width)),
            whole((ENC, width)),
            whole((KW, ENC)),
        ],
        out_shape=[
            jax.ShapeDtypeStruct((tokens, width), BF16),
            jax.ShapeDtypeStruct((tokens, width), BF16),
            jax.ShapeDtypeStruct((spans * NBR, NLEN, ENC), BF16),
            jax.ShapeDtypeStruct((ENC, width), BF16),
            jax.ShapeDtypeStruct((ENC, width), BF16),
            jax.ShapeDtypeStruct((KW, ENC), F32),
        ],
        scratch_shapes=[
            pltpu.VMEM((ENC, 2 * width), BF16),
            pltpu.VMEM((NBR * NLEN, ENC), BF16),
            pltpu.VMEM((ENC, keys_all), BF16),
            pltpu.VMEM((keys_all, 2 * width), BF16),
            pltpu.VMEM((NBR * NLEN, ENC), F32),
            pltpu.VMEM((KW, 8, ENC), F32),
        ],
        compiler_params=pltpu.CompilerParams(
            dimension_semantics=("arbitrary",), vmem_limit_bytes=56 * 1024 * 1024
        ),
        cost_estimate=pl.CostEstimate(
            flops=27_000_000_000, bytes_accessed=30_000_000, transcendentals=1_200_000
        ),
    )(queries, cotangent, raw, key_weight, value_weight, conv_kernel)


def shards(
    queries, cotangent, db_states, key_weight, value_weight, conv_kernel, nbr_owner, nbr_row
):
    owners = lax.axis_size("dp")
    span_count = nbr_owner.shape[0]
    request_count = span_count * NBR
    capacity = max(2, (request_count + owners - 1) // owners)
    quarter = db_states.shape[1]
    local_blocks = db_states.shape[0]
    slots_total = owners * capacity
    owner_flat = nbr_owner.reshape(request_count)
    row_flat = nbr_row.reshape(request_count)
    positions = jnp.arange(request_count, dtype=jnp.int32)
    same_owner = owner_flat[:, None] == owner_flat[None, :]
    earlier = positions[:, None] > positions[None, :]
    slot_index = jnp.sum(jnp.logical_and(same_owner, earlier).astype(jnp.int32), axis=1)
    target = owner_flat * capacity + slot_index
    slot_hits = target[:, None] == jnp.arange(slots_total, dtype=jnp.int32)[None, :]
    used_slot = jnp.any(slot_hits, axis=0)
    row_sent = jnp.sum(jnp.where(slot_hits, row_flat[:, None], 0), axis=0)
    row_table = jnp.where(used_slot, row_sent, -1).reshape(owners, capacity)
    slot_matrix = slot_hits.astype(jnp.bfloat16)
    states_flat = db_states.reshape(local_blocks, quarter * ENC)
    asked = lax.all_to_all(row_table, "dp", split_axis=0, concat_axis=0, tiled=True)
    asked_flat = asked.reshape(slots_total)
    picker = (asked_flat[:, None] == jnp.arange(local_blocks, dtype=jnp.int32)[None, :]).astype(
        jnp.bfloat16
    )
    fetched = jnp.dot(picker, states_flat, preferred_element_type=jnp.float32).astype(jnp.bfloat16)
    fetched = fetched.reshape(owners, capacity, quarter, ENC)
    replied = lax.all_to_all(fetched, "dp", split_axis=0, concat_axis=0, tiled=True)
    received = jnp.dot(
        slot_matrix, replied.reshape(slots_total, quarter * ENC), preferred_element_type=jnp.float32
    )
    received = received.astype(jnp.bfloat16).reshape(request_count, quarter, ENC)
    raw = lax.all_gather(received, "db", axis=1, tiled=True)
    attended, grad_query, part, key_term, value_term, taps_term = core(
        queries, cotangent, raw, key_weight, value_weight, conv_kernel
    )
    grad_raw = lax.psum_scatter(part, "db", scatter_dimension=1, tiled=True)
    grad_raw_b = grad_raw.reshape(request_count, quarter * ENC)
    grad_send = jnp.einsum(
        "ns,nf->sf", slot_matrix, grad_raw_b, preferred_element_type=jnp.float32
    ).astype(jnp.bfloat16)
    grad_send = grad_send.reshape(owners, capacity, quarter, ENC)
    grad_back = lax.all_to_all(grad_send, "dp", split_axis=0, concat_axis=0, tiled=True)
    picker_back = (
        jnp.arange(local_blocks, dtype=jnp.int32)[:, None] == asked_flat[None, :]
    ).astype(jnp.bfloat16)
    grad_states = jnp.dot(
        picker_back,
        grad_back.reshape(slots_total, quarter * ENC),
        preferred_element_type=jnp.float32,
    )
    grad_states = grad_states.reshape(local_blocks, quarter, ENC)
    grad_key_weight, grad_value_weight = lax.psum((key_term, value_term), "dp")
    grad_kernel = lax.psum(taps_term, ("dp", "db"))
    return (
        attended,
        grad_query,
        grad_states,
        grad_key_weight.astype(F32),
        grad_value_weight.astype(F32),
        grad_kernel,
    )


def solution(mesh):
    return jax.shard_map(
        shards,
        mesh=mesh,
        in_specs=(
            P("dp", "db"),
            P("dp", "db"),
            P("dp", "db", None),
            P(None, "db"),
            P(None, "db"),
            P(),
            P("dp", None),
            P("dp", None),
        ),
        out_specs=(
            P("dp", "db"),
            P("dp", "db"),
            P("dp", "db", None),
            P(None, "db"),
            P(None, "db"),
            P(),
        ),
        check_vma=False,
    )
```

time: 494 us -> 440 us (0.89); the launches traced: 488 us -> 440 us
  Pallas kernels: 0 us -> 95.2 us
  matrix products: 101 us -> 7.39 us
  waiting for transfers between devices: 162 us -> 129 us
  local copies, waits for them, and re-layouts: 48.1 us -> 16.4 us
  blocking collectives: 124 us -> 153 us
  starting transfers between devices: 28.9 us -> 17.4 us
    pallas_call x0 -> x1, Pallas kernels: none -> 95.2 us  [core(): pl.pallas_call(functools.partial(core_kernel, heads), grid=(spans,), in_s...]
    dot_general x12 -> x0, matrix products: 92.1 us -> none  [the longest x1 15.7 us: shards(): jnp.einsum('chqk,cqhd->ckhd', probs_b, grad_heads, preferred_element_type...]
    reduce_scatter x1, waiting for transfers between devices: 80 us -> 46.9 us  [shards(): grad_raw = lax.psum_scatter(part, 'db', scatter_dimension=1, tiled=True)]
    psum x1, blocking collectives: 74.7 us -> 105 us  [shards(): grad_kernel = lax.psum(taps_term, ('dp', 'db'))]
    unnamed x54 -> x14, local copies, waits for them, and re-layouts: 32.2 us -> 13.9 us
    convert_element_type x4 -> x0, local copies, waits for them, and re-layouts: 10.9 us -> none  [the longest x1 5.74 us: shards(): grad_values = jnp.einsum('chqk,cqhd->ckhd', probs_b, grad_heads, preferre...]
    ppermute x4 -> x0, starting transfers between devices: 10.4 us -> none  [the longest x2 7.87 us: extended(): lax.ppermute(lax.slice_in_dim(block, block.shape[dim] - width, None, axis...]
  transfers between devices with their start and end apart: 9 -> 5, of which waited for: 5 -> 4; matrix products, arithmetic and copies ran while one was open for 12% -> 2% of each run, Pallas kernels for 0% -> 0%
where the time goes in v1:
time: 440 us
  blocking collectives  153 us (35%)
  waiting for transfers between devices  129 us (29%)
  Pallas kernels  95.2 us (22%)
  starting transfers between devices  17.4 us (4%)
  local copies, waits for them, and re-layouts  16.4 us (4%)
  between operations  13.9 us (3%)
  matrix products  7.39 us (2%)
  other arithmetic  7.19 us (2%)
    psum x1, blocking collectives, shards(): grad_kernel = lax.psum(taps_term, ('dp', 'db'))  105 us
    pallas_call x1, Pallas kernels, core(): pl.pallas_call(functools.partial(core_kernel, heads), grid=(spans,), in_s...  95.2 us
    all_to_all x1, blocking collectives, shards(): lax.all_to_all(fetched, 'dp', split_axis=0, concat_axis=0, tiled=True)  49 us
    reduce_scatter x1, waiting for transfers between devices, shards(): grad_raw = lax.psum_scatter(part, 'db', scatter_dimension=1, tiled=True)  46.9 us
    all_gather x1, waiting for transfers between devices, shards(): raw = lax.all_gather(received, 'db', axis=1, tiled=True)  45.2 us
    psum x1, waiting for transfers between devices, shards(): grad_key_weight, grad_value_weight = lax.psum((key_term, value_term), 'dp')  31.1 us
    unnamed x14, local copies, waits for them, and re-layouts  13.9 us
    all_to_all x1, starting transfers between devices, shards(): lax.all_to_all(row_table, 'dp', split_axis=0, concat_axis=0, tiled=True)  9.43 us
  transfers between devices with their start and end apart: 5, of which 4 were waited for; matrix products, arithmetic and copies ran while one was open for 2% of the time, Pallas kernels for 0%

profile of v1, /device:TPU:1, one launch (start us, length us, event | category | flops | bytes accessed | tf_op | source)
XLA Modules:
  0.0 439.6 jit_solution(9220161308552230599)
XLA Ops:
  7.2 0.8 copy.26
  8.0 0.2 convert_reduce_fusion
  8.3 0.8 copy.27
  9.3 0.7 select_n.21
  10.0 9.4 %all-to-all-start = ((s32[32,1,2]{2,1,0:T(1,128)}), s32[32,1,2]{2,1,0:T(1,128)S(1)}, u32[]{:S(2)}, u32[]{:S(2)}) async-start(s32[32,1,2]{2,1,0:T(1,128)} %bitcast), calls=%async_computation | async-start | bytes 32768 | tf_op jit(solution)/shard_map/all_to_all | solution.py:211
  19.5 2.1 copy.32
  21.6 4.7 %all-to-all-done = s32[32,1,2]{2,1,0:T(1,128)S(1)} async-done(((s32[32,1,2]{2,1,0:T(1,128)}), s32[32,1,2]{2,1,0:T(1,128)S(1)}, u32[]{:S(2)}, u32[]{:S(2)}) %all-to-all-start) | async-done | bytes 288 | tf_op jit(solution)/shard_map/all_to_all | solution.py:211
  26.3 0.5 broadcast.22
  26.8 0.7 reduce.3
  27.6 1.2 convolution_convert_fusion.1
  28.8 0.6 copy.33
  29.3 49.0 %all_to_all.16 = bf16[32,2,32,896]{3,2,1,0:T(8,128)(2,1)S(1)} all-to-all(bf16[32,2,32,896]{3,2,1,0:T(8,128)(2,1)S(1)} %bitcast.37), channel_id=1, replica_groups=mesh['dp'=32,'db'=4] {'dp'}, dimensions={0} | all-to-all | bytes 7340032 | tf_op jit(solution)/shard_map/all_to_all | solution.py:218
  78.3 1.4 copy.34
  79.7 0.7 convolution_convert_fusion.2
  80.4 0.2 copy.35
  80.6 1.0 slice
  81.6 0.2 reduce-scatter.2.cloned.1.call-start
  81.9 45.2 %all-gather.2.cloned.1.call-done.raw_ref = bf16[18,128,896]{2,1,0:T(8,128)(2,1)} async-done(((bf16[18,32,896]{2,1,0:T(8,128)(2,1)}), bf16[18,128,896]{2,1,0:T(8,128)(2,1)}) %all-gather.2.cloned.1.call-update) | async-done | bytes 4128784 | tf_op jit(solution)/shard_map/all_gather | solution.py:223
  127.1 95.2 %shard_map.127 = (bf16[576,1024]{1,0:T(8,128)(2,1)}, bf16[576,1024]{1,0:T(8,128)(2,1)}, bf16[18,128,896]{2,1,0:T(8,128)(2,1)}, bf16[896,1024]{1,0:T(8,128)(2,1)}...) custom-call(bf16[576,1024]{1,0:T(8,128)(2,1)} %q_ref.1, bf16[576,1024]{1,0:T(8,128)(2,1)} %g_ref.1, ...), custom_call_target="tpu_custom_call" | custom-call | flops 27000000512 | bytes 30000000 | tf_op jit(solution)/shard_map/pallas_call | solution.py:144
  222.3 46.9 %reduce-scatter.2.cloned.1.call-done = bf16[18,32,896]{2,1,0:T(8,128)(2,1)} async-done(((bf16[18,128,896]{2,1,0:T(8,128)(2,1)}), bf16[18,32,896]{2,1,0:T(8,128)(2,1)}) %reduce-scatter.2.cloned.1.call-update) | async-done | bytes 1032208 | tf_op jit(solution)/shard_map/reduce_scatter | solution.py:227
  269.1 1.3 pad
  270.4 0.4 copy.36
  270.9 1.2 convolution_convert_fusion
  272.1 2.4 copy.37
  274.5 7.7 %all-to-all-start.2 = ((bf16[32,2,32,896]{3,2,1,0:T(8,128)(2,1)}), bf16[32,2,32,896]{3,2,1,0:T(8,128)(2,1)}, u32[]{:S(2)}, u32[]{:S(2)}) async-start(bf16[32,2,32,896]{3,2,1,0:T(8,128)(2,1)} %bitcast.36), calls=%async_computation.3 | async-start | bytes 7340032 | tf_op jit(solution)/shard_map/all_to_all | solution.py:233
  282.3 0.7 all-reduce.3.cloned.1.call-update
  283.0 104.5 %psum.23 = f32[3,896]{1,0:T(4,128)} all-reduce(f32[3,896]{1,0:T(4,128)S(1)} %copy-done.1), channel_id=1, replica_groups=mesh['dp'=32,'db'=4] {'dp','db'}, use_global_device_ids=true, to_apply=%region_6.7 | all-reduce | flops 2688 | bytes 21504 | tf_op jit(solution)/shard_map/psum | solution.py:244
  387.5 31.1 %all-reduce.3.cloned.1.call-done = (bf16[896,1024]{1,0:T(8,128)(2,1)}, bf16[896,1024]{1,0:T(8,128)(2,1)}) async-done(((bf16[896,1024]{1,0:T(8,128)(2,1)}, bf16[896,1024]{1,0:T(8,128)(2,1)}), (bf16[896,1024]{1,0:T(8,128)(2,1)}, bf16[896,1024]{1,0:T(8,128)(2,1)})) %all-reduce.3.cloned.1.call-update) | async-done | bytes 3670032 | tf_op jit(solution)/shard_map/psum | solution.py:243
  418.6 3.9 convert_element_type.25
  422.5 2.3 convert_element_type.26
  424.8 4.3 fusion
  429.1 4.0 copy.30
  (16 shorter events, 0.6 us)
Async XLA Ops:
  10.0 16.3 %all-to-all-start = ((s32[32,1,2]{2,1,0:T(1,128)}), s32[32,1,2]{2,1,0:T(1,128)S(1)}, u32[]{:S(2)}, u32[]{:S(2)}) async-start(s32[32,1,2]{2,1,0:T(1,128)} %bitcast), calls=%async_computation | async-start | bytes 32768 | tf_op jit(solution)/shard_map/all_to_all | solution.py:211
  19.4 107.7 %all-gather.2.cloned.1.call-start = ((), (), s32[]{:S(2)}) async-start(), calls=%async_computation.4 | async-start | bytes 5160960 | tf_op jit(solution)/shard_map/all_gather | solution.py:223
  81.6 187.5 %reduce-scatter.2.cloned.1.call-start = ((), (), s32[]{:S(2)}) async-start(), calls=%async_computation.5 | async-start | bytes 5160960 | tf_op jit(solution)/shard_map/reduce_scatter | solution.py:227
  274.5 150.2 %all-to-all-start.2 = ((bf16[32,2,32,896]{3,2,1,0:T(8,128)(2,1)}), bf16[32,2,32,896]{3,2,1,0:T(8,128)(2,1)}, u32[]{:S(2)}, u32[]{:S(2)}) async-start(bf16[32,2,32,896]{3,2,1,0:T(8,128)(2,1)} %bitcast.36), calls=%async_computation.3 | async-start | bytes 7340032 | tf_op jit(solution)/shard_map/all_to_all | solution.py:233
  282.2 0.8 copy-start.1
  282.2 136.4 %all-reduce.3.cloned.1.call-start = ((), (), s32[]{:S(2)}) async-start(), calls=%async_computation.6 | async-start | bytes 7340032 | tf_op jit(solution)/shard_map/psum | solution.py:243
  418.6 3.9 copy-start
Sparse Core Ops, SparseCore 0:
  81.7 45.2 all-gather.1
  222.4 46.6 reduce-scatter.1
  287.5 131.0 all-reduce.2

commit v2 on v1

--- a/solution.py
+++ b/solution.py
@@ -49,6 +49,9 @@
     grads,
     gm_s,
     taps_acc,
+    kv_s,
+    both_s,
+    stacked_s,
 ):
     span = pl.program_id(0)
     scale = 1.0 / math.sqrt(HD)
@@ -64,7 +67,7 @@
     for c in range(CHUNKS):
         cols = slice(c * LANES, (c + 1) * LANES)
         for n in range(NBR):
-            raw = raw_ref[n, :, cols].astype(F32)
+            raw = raw_ref[c, :, n].reshape(NLEN, LANES).astype(F32)
             down, up = shifted(raw)
             mixed = taps_ref[0:1, cols] * down
             mixed = mixed + taps_ref[1:2, cols] * raw
@@ -75,28 +78,37 @@
     mixed_t[:, rows] = mixed.T
 
     zeros = jnp.zeros((SPAN, HD), BF16)
+    kv_s[...] = jnp.dot(mixed, weights[...], preferred_element_type=F32).astype(BF16)
+
+    def diag(h):
+        q = q_ref[:, h * HD : (h + 1) * HD]
+        g = g_ref[:, h * HD : (h + 1) * HD]
+        return jnp.concatenate(
+            [jnp.concatenate([q, zeros], axis=1), jnp.concatenate([zeros, g], axis=1)], axis=0
+        )
+
     for h in range(heads):
         wide = slice(2 * h * HD, (2 * h + 2) * HD)
-        cols = slice(h * HD, (h + 1) * HD)
-        kv = jnp.dot(mixed, weights[:, wide], preferred_element_type=F32).astype(BF16)
-        q = q_ref[:, cols]
-        g = g_ref[:, cols]
-        block_diag = jnp.concatenate(
-            [jnp.concatenate([q, zeros], axis=1), jnp.concatenate([zeros, g], axis=1)], axis=0
-        )
-        both = lax.dot_general(block_diag, kv, NT, preferred_element_type=F32)
-        scores = both[:SPAN] * scale
-        grad_probs = both[SPAN:]
+        both_s[h] = lax.dot_general(diag(h), kv_s[:, wide], NT, preferred_element_type=F32)
+    for h in range(heads):
+        scores = both_s[h, :SPAN] * scale
+        grad_probs = both_s[h, SPAN:]
         expo = jnp.exp(scores - jnp.max(scores, axis=-1, keepdims=True))
         probs = expo / jnp.sum(expo, axis=-1, keepdims=True)
         inner = jnp.sum(grad_probs * probs, axis=-1, keepdims=True)
         grad_scores = scale * probs * (grad_probs - inner)
-        stacked = jnp.concatenate([grad_scores, probs], axis=0).astype(BF16)
-        out = jnp.dot(stacked, kv, preferred_element_type=F32)
+        stacked_s[h, :SPAN] = grad_scores.astype(BF16)
+        stacked_s[h, SPAN:] = probs.astype(BF16)
+    for h in range(heads):
+        wide = slice(2 * h * HD, (2 * h + 2) * HD)
+        cols = slice(h * HD, (h + 1) * HD)
+        out = jnp.dot(stacked_s[h], kv_s[:, wide], preferred_element_type=F32)
         gq_ref[:, cols] = out[:SPAN, :HD].astype(BF16)
         att_ref[:, cols] = out[SPAN:, HD:].astype(BF16)
-        grads[rows, wide] = jnp.dot(
-            stacked.T, block_diag, preferred_element_type=F32
+    for h in range(heads):
+        wide = slice(2 * h * HD, (2 * h + 2) * HD)
+        grads[rows, wide] = lax.dot_general(
+            stacked_s[h], diag(h), (((0,), (0,)), ((), ())), preferred_element_type=F32
         ).astype(BF16)
 
     gm_s[...] = lax.dot_general(grads[rows, :], weights[...], NT, preferred_element_type=F32)
@@ -108,8 +120,8 @@
             back = taps_ref[0:1, cols] * gm_up
             back = back + taps_ref[1:2, cols] * gm
             back = back + taps_ref[2:3, cols] * gm_down
-            part_ref[n, :, cols] = back.astype(BF16)
-            raw = raw_ref[n, :, cols].astype(F32)
+            part_ref[c, :, n] = back.astype(BF16).reshape(part_ref.shape[1], -1, LANES)
+            raw = raw_ref[c, :, n].reshape(NLEN, LANES).astype(F32)
             down, up = shifted(raw)
             for w, other in enumerate((down, raw, up)):
                 taps_acc[w, :, cols] += jnp.sum(
@@ -140,7 +152,8 @@
         shape, lambda i: (0,) * len(shape), pipeline_mode=pl.Buffered(1)
     )
     span_rows = pl.BlockSpec((SPAN, width), lambda i: (i, 0))
-    blocks = pl.BlockSpec((NBR, NLEN, ENC), lambda i: (i, 0, 0))
+    parts, quarter = raw.shape[1], raw.shape[3]
+    blocks = pl.BlockSpec((CHUNKS, parts, NBR, quarter, LANES), lambda i: (0, 0, i, 0, 0))
     return pl.pallas_call(
         functools.partial(core_kernel, heads),
         grid=(spans,),
@@ -163,7 +176,7 @@
         out_shape=[
             jax.ShapeDtypeStruct((tokens, width), BF16),
             jax.ShapeDtypeStruct((tokens, width), BF16),
-            jax.ShapeDtypeStruct((spans * NBR, NLEN, ENC), BF16),
+            jax.ShapeDtypeStruct(raw.shape, BF16),
             jax.ShapeDtypeStruct((ENC, width), BF16),
             jax.ShapeDtypeStruct((ENC, width), BF16),
             jax.ShapeDtypeStruct((KW, ENC), F32),
@@ -175,6 +188,9 @@
             pltpu.VMEM((keys_all, 2 * width), BF16),
             pltpu.VMEM((NBR * NLEN, ENC), F32),
             pltpu.VMEM((KW, 8, ENC), F32),
+            pltpu.VMEM((NBR * NLEN, 2 * width), BF16),
+            pltpu.VMEM((heads, 2 * SPAN, NBR * NLEN), F32),
+            pltpu.VMEM((heads, 2 * SPAN, NBR * NLEN), BF16),
         ],
         compiler_params=pltpu.CompilerParams(
             dimension_semantics=("arbitrary",), vmem_limit_bytes=56 * 1024 * 1024
@@ -183,6 +199,167 @@
             flops=27_000_000_000, bytes_accessed=30_000_000, transcendentals=1_200_000
         ),
     )(queries, cotangent, raw, key_weight, value_weight, conv_kernel)
+
+
+def dp_peer(step):
+    me = lax.axis_index("dp")
+    z = lax.rem(me // 8 + step // 8, 4)
+    x = lax.rem(lax.rem(me // 2, 4) + lax.rem(step // 2, 4), 4)
+    return z * 8 + x * 2 + lax.rem(me + step, 2)
+
+
+def fetch_kernel(
+    owners,
+    parts,
+    slot_ref,
+    table_ref,
+    states_ref,
+    raw_ref,
+    asked_ref,
+    asked_s,
+    send,
+    ask_sem,
+    local_sem,
+    send_sem,
+    recv_sem,
+    y_send,
+    y_recv,
+    *recv,
+):
+    me = lax.axis_index("dp")
+    y = lax.axis_index("db")
+    right = lax.rem(y + 1, parts)
+    left = lax.rem(y + parts - 1, parts)
+    requests = raw_ref.shape[2]
+    half = requests // 2
+    capacity = 2
+    others = owners - 1
+
+    barrier = pltpu.get_barrier_semaphore()
+
+    def greet(step, carry):
+        pl.semaphore_signal(barrier, inc=1, device_id={"dp": dp_peer(step)})
+        return carry
+
+    lax.fori_loop(1, owners, greet, 0)
+    for side in (left, right):
+        pl.semaphore_signal(barrier, inc=1, device_id={"db": side})
+    pl.semaphore_wait(barrier, others + 2)
+
+    def ask(step, carry):
+        peer = dp_peer(step)
+        pltpu.make_async_remote_copy(
+            src_ref=table_ref.at[peer],
+            dst_ref=asked_ref.at[me],
+            send_sem=ask_sem.at[0],
+            recv_sem=ask_sem.at[1],
+            device_id={"dp": peer},
+        ).start()
+        return carry
+
+    lax.fori_loop(1, owners, ask, 0)
+    asked_ref[me] = table_ref[me]
+    most = asked_ref.at[pl.ds(0, others)]
+    pltpu.make_async_copy(most, most, ask_sem.at[1]).wait()
+    pltpu.make_async_copy(asked_ref, asked_s, local_sem).start()
+    pltpu.make_async_copy(asked_ref, asked_s, local_sem).wait()
+
+    for c in range(CHUNKS):
+        cols = slice(c * LANES, (c + 1) * LANES)
+
+        def reply(step, carry):
+            peer = dp_peer(step)
+            for k in range(capacity):
+                row = jnp.maximum(asked_s[peer, 0, k], 0)
+                send[c, capacity * peer + k] = states_ref[row, :, cols]
+            pltpu.make_async_remote_copy(
+                src_ref=send.at[c, pl.ds(capacity * peer, capacity)],
+                dst_ref=recv[c].at[pl.ds(capacity * me, capacity)],
+                send_sem=send_sem.at[c],
+                recv_sem=recv_sem.at[c],
+                device_id={"dp": peer},
+            ).start()
+            return carry
+
+        lax.fori_loop(1, owners, reply, 0)
+        for k in range(capacity):
+            row = jnp.maximum(asked_s[me, 0, k], 0)
+            recv[c][capacity * me + k] = states_ref[row, :, cols]
+
+    def along_y(kind, c, part, rows, side):
+        block = raw_ref.at[c, part, rows]
+        return pltpu.make_async_remote_copy(
+            src_ref=block,
+            dst_ref=block,
+            send_sem=y_send.at[kind, c],
+            recv_sem=y_recv.at[kind, c],
+            device_id={"db": side},
+        )
+
+    everything, low, high = pl.ds(0, requests), pl.ds(0, half), pl.ds(half, requests - half)
+
+    def arrivals(kind, c):
+        far = lax.rem(y + 2, parts)
+        part, rows = ((left, everything), (right, everything), (far, low), (far, high))[kind]
+        return along_y(kind, c, part, rows, right)
+
+    for c in range(CHUNKS + 1):
+        if c < CHUNKS:
+            most = recv[c].at[pl.ds(0, capacity * others)]
+            pltpu.make_async_copy(most, most, recv_sem.at[c]).wait()
+            for p in range(requests):
+                raw_ref[c, y, p] = recv[c][slot_ref[p]]
+            along_y(0, c, y, everything, right).start()
+            along_y(1, c, y, everything, left).start()
+        if c >= 1:
+            arrivals(0, c - 1).wait_recv()
+            along_y(2, c - 1, left, low, right).start()
+            arrivals(1, c - 1).wait_recv()
+            along_y(3, c - 1, right, high, left).start()
+    for c in range(CHUNKS):
+        arrivals(2, c).wait_recv()
+        arrivals(3, c).wait_recv()
+        along_y(0, c, y, everything, right).wait_send()
+        along_y(1, c, y, everything, left).wait_send()
+        along_y(2, c, left, low, right).wait_send()
+        along_y(3, c, right, high, left).wait_send()
+        most = send.at[c, pl.ds(0, capacity * others)]
+        pltpu.make_async_copy(most, most, send_sem.at[c]).wait()
+    most = table_ref.at[pl.ds(0, others)]
+    pltpu.make_async_copy(most, most, ask_sem.at[0]).wait()
+
+
+def fetch(slots, table, states):
+    owners = table.shape[0]
+    parts = lax.axis_size("db")
+    requests = slots.shape[0]
+    quarter = states.shape[1]
+    vmem = pl.BlockSpec(memory_space=pltpu.VMEM)
+    dma = pltpu.SemaphoreType.DMA
+    return pl.pallas_call(
+        functools.partial(fetch_kernel, owners, parts),
+        in_specs=[pl.BlockSpec(memory_space=pltpu.SMEM), vmem, vmem],
+        out_specs=[vmem, vmem],
+        out_shape=[
+            jax.ShapeDtypeStruct((CHUNKS, parts, requests, quarter, LANES), BF16),
+            jax.ShapeDtypeStruct(table.shape, jnp.int32),
+        ],
+        scratch_shapes=[
+            pltpu.SMEM(table.shape, jnp.int32),
+            pltpu.VMEM((CHUNKS, 2 * owners, quarter, LANES), BF16),
+            dma((2,)),
+            dma,
+            dma((CHUNKS,)),
+            dma((CHUNKS,)),
+            dma((4, CHUNKS)),
+            dma((4, CHUNKS)),
+        ]
+        + [pltpu.VMEM((2 * owners, quarter, LANES), BF16)] * CHUNKS,
+        compiler_params=pltpu.CompilerParams(
+            collective_id=0, has_side_effects=True, vmem_limit_bytes=40 * 1024 * 1024
+        ),
+        cost_estimate=pl.CostEstimate(flops=0, bytes_accessed=16_000_000, transcendentals=0),
+    )(slots, table, states)
 
 
 def shards(
@@ -207,24 +384,14 @@
     row_sent = jnp.sum(jnp.where(slot_hits, row_flat[:, None], 0), axis=0)
     row_table = jnp.where(used_slot, row_sent, -1).reshape(owners, capacity)
     slot_matrix = slot_hits.astype(jnp.bfloat16)
-    states_flat = db_states.reshape(local_blocks, quarter * ENC)
-    asked = lax.all_to_all(row_table, "dp", split_axis=0, concat_axis=0, tiled=True)
-    asked_flat = asked.reshape(slots_total)
-    picker = (asked_flat[:, None] == jnp.arange(local_blocks, dtype=jnp.int32)[None, :]).astype(
-        jnp.bfloat16
-    )
-    fetched = jnp.dot(picker, states_flat, preferred_element_type=jnp.float32).astype(jnp.bfloat16)
-    fetched = fetched.reshape(owners, capacity, quarter, ENC)
-    replied = lax.all_to_all(fetched, "dp", split_axis=0, concat_axis=0, tiled=True)
-    received = jnp.dot(
-        slot_matrix, replied.reshape(slots_total, quarter * ENC), preferred_element_type=jnp.float32
-    )
-    received = received.astype(jnp.bfloat16).reshape(request_count, quarter, ENC)
-    raw = lax.all_gather(received, "db", axis=1, tiled=True)
+    table = jnp.pad(row_table[:, None, :], ((0, 0), (0, 0), (0, LANES - capacity)))
+    raw, asked = fetch(target, table, db_states)
+    asked_flat = asked[:, 0, :capacity].reshape(slots_total)
     attended, grad_query, part, key_term, value_term, taps_term = core(
         queries, cotangent, raw, key_weight, value_weight, conv_kernel
     )
     grad_raw = lax.psum_scatter(part, "db", scatter_dimension=1, tiled=True)
+    grad_raw = jnp.transpose(grad_raw.reshape(CHUNKS, request_count, quarter, LANES), (1, 2, 0, 3))
     grad_raw_b = grad_raw.reshape(request_count, quarter * ENC)
     grad_send = jnp.einsum(
         "ns,nf->sf", slot_matrix, grad_raw_b, preferred_element_type=jnp.float32

time: 440 us -> 398 us (0.905)
  blocking collectives: 153 us -> 105 us
  Pallas kernels: 95.2 us -> 119 us
  starting transfers between devices: 17.4 us -> 7.8 us
  waiting for transfers between devices: 129 us -> 122 us
    unnamed x3, waiting for transfers between devices: 0.71 us -> 91.2 us
    pallas_call x0 -> x1, Pallas kernels: none -> 66.1 us  [fetch(): pl.pallas_call(functools.partial(fetch_kernel, owners, parts), in_specs=[...]
    all_to_all x1 -> x0, blocking collectives: 49 us -> none  [shards(): lax.all_to_all(fetched, 'dp', split_axis=0, concat_axis=0, tiled=True)]
    reduce_scatter x1 -> x0, waiting for transfers between devices: 46.9 us -> none  [shards(): grad_raw = lax.psum_scatter(part, 'db', scatter_dimension=1, tiled=True)]
    all_gather x1 -> x0, waiting for transfers between devices: 45.2 us -> none  [shards(): raw = lax.all_gather(received, 'db', axis=1, tiled=True)]
    pallas_call x1, Pallas kernels: 95.2 us -> 52.4 us  [core(): pl.pallas_call(functools.partial(core_kernel, heads), grid=(spans,), in_s...]
    all_to_all x1 -> x0, starting transfers between devices: 9.43 us -> none  [shards(): lax.all_to_all(row_table, 'dp', split_axis=0, concat_axis=0, tiled=True)]
    all_to_all x1 -> x0, waiting for transfers between devices: 4.72 us -> none  [shards(): lax.all_to_all(row_table, 'dp', split_axis=0, concat_axis=0, tiled=True)]
  transfers between devices with their start and end apart: 5 -> 3, of which waited for: 4 -> 2; matrix products, arithmetic and copies ran while one was open for 2% -> 2% of each run, Pallas kernels for 0% -> 0%
where the time goes in v2:
time: 398 us; the launch traced here: 397 us
  waiting for transfers between devices  122 us (31%)
  Pallas kernels  119 us (30%)
  blocking collectives  105 us (26%)
  local copies, waits for them, and re-layouts  16.7 us (4%)
  between operations  15.6 us (4%)
  starting transfers between devices  7.8 us (2%)
  other arithmetic  6.51 us (2%)
  matrix products  5.56 us (1%)
    psum x1, blocking collectives, shards(): grad_kernel = lax.psum(taps_term, ('dp', 'db'))  105 us
    unnamed x3, waiting for transfers between devices  91.2 us
    pallas_call x1, Pallas kernels, fetch(): pl.pallas_call(functools.partial(fetch_kernel, owners, parts), in_specs=[...  66.1 us
    pallas_call x1, Pallas kernels, core(): pl.pallas_call(functools.partial(core_kernel, heads), grid=(spans,), in_s...  52.4 us
    psum x1, waiting for transfers between devices, shards(): grad_key_weight, grad_value_weight = lax.psum((key_term, value_term), 'dp')  30.8 us
    unnamed x15, local copies, waits for them, and re-layouts  12.6 us
  transfers between devices with their start and end apart: 3, of which 2 were waited for; matrix products, arithmetic and copies ran while one was open for 2% of the time, Pallas kernels for 0%

profile of v2, /device:TPU:1, one launch (start us, length us, event | category | flops | bytes accessed | tf_op | source)
XLA Modules:
  0.0 397.3 jit_solution(9654619055797186547)
XLA Ops:
  8.0 0.0 all-reduce.6.cloned.1.call-start
  8.0 0.8 copy.30
  8.8 0.1 reshape.60
  8.9 0.2 convert_reduce_fusion
  9.1 0.1 fusion.5
  9.2 0.8 copy.31
  10.0 0.1 broadcast_in_dim.23
  10.0 0.1 select_reduce_fusion
  10.1 0.1 select_n.20
  10.3 1.5 copy-done
  11.8 66.1 %shard_map.127 = (bf16[7,4,18,32,128]{4,3,2,1,0:T(8,128)(2,1)S(1)}, s32[32,1,128]{2,1,0:T(1,128)S(1)}) custom-call(s32[18]{0:T(128)S(1)} %multiply_add_fusion.slot_ref, s32[32,1,128]{2,1,0:T(1,128)S(1)} %pad.4.table_ref, bf16[32,32,896]{2,1,0:T(8,128)(2,1)S(1)} %copy-done), custom_call_target="tpu_custom_call" | custom-call | bytes 16000000 | tf_op jit(solution)/shard_map/pallas_call | solution.py:339
  77.9 1.9 copy-done.1
  79.8 52.4 %shard_map.128 = (bf16[576,1024]{1,0:T(8,128)(2,1)}, bf16[576,1024]{1,0:T(8,128)(2,1)}, bf16[7,4,18,32,128]{4,3,2,1,0:T(8,128)(2,1)}, bf16[896,1024]{1,0:T(8,128...) custom-call(bf16[576,1024]{1,0:T(8,128)(2,1)} %q_ref.1, bf16[576,1024]{1,0:T(8,128)(2,1)} %g_ref.1, ...), custom_call_target="tpu_custom_call" | custom-call | flops 27000000512 | bytes 30000000 | tf_op jit(solution)/shard_map/pallas_call | solution.py:157
  132.3 0.0 all-reduce.6.cloned.1.call-update
  132.3 0.6 copy-done.4
  132.9 0.6 dynamic-slice
  133.5 90.7 %all-reduce.6.cloned.1.call-done = bf16[7,4,18,32,128]{4,3,2,1,0:T(8,128)(2,1)} async-done(((bf16[7,4,18,32,128]{4,3,2,1,0:T(8,128)(2,1)}), bf16[7,4,18,32,128]{4,3,2,1,0:T(8,128)(2,1)}) %all-reduce.6.cloned.1.call-update) | async-done | bytes 4128784
  224.2 1.9 dynamic-slice_bitcast_fusion
  226.2 0.7 copy.33
  226.8 1.1 reshape.62
  228.0 1.2 convolution_convert_fusion
  229.2 2.4 copy.39
  231.6 7.7 %all-to-all-start = ((bf16[32,2,32,896]{3,2,1,0:T(8,128)(2,1)}), bf16[32,2,32,896]{3,2,1,0:T(8,128)(2,1)}, u32[]{:S(2)}, u32[]{:S(2)}) async-start(bf16[32,2,32,896]{3,2,1,0:T(8,128)(2,1)} %bitcast.31), calls=%async_computation | async-start | bytes 7340032 | tf_op jit(solution)/shard_map/all_to_all | solution.py:400
  239.3 0.0 all-reduce.8.cloned.1.call-start
  239.4 0.5 all-reduce.8.cloned.1.call-update
  240.0 0.1 eq.48
  240.1 104.6 %psum.23 = f32[3,896]{1,0:T(4,128)} all-reduce(f32[3,896]{1,0:T(4,128)S(1)} %copy-done.3), channel_id=1, replica_groups=mesh['dp'=32,'db'=4] {'dp','db'}, use_global_device_ids=true, to_apply=%region_6.7 | all-reduce | flops 2688 | bytes 21504 | tf_op jit(solution)/shard_map/psum | solution.py:411
  344.7 30.8 %all-reduce.8.cloned.1.call-done = (bf16[896,1024]{1,0:T(8,128)(2,1)}, bf16[896,1024]{1,0:T(8,128)(2,1)}) async-done(((bf16[896,1024]{1,0:T(8,128)(2,1)}, bf16[896,1024]{1,0:T(8,128)(2,1)}), (bf16[896,1024]{1,0:T(8,128)(2,1)}, bf16[896,1024]{1,0:T(8,128)(2,1)})) %all-reduce.8.cloned.1.call-update) | async-done | bytes 3670032 | tf_op jit(solution)/shard_map/psum | solution.py:410
  375.4 3.9 convert_element_type.16
  379.3 2.3 convert_element_type.17
  381.6 4.3 %fusion = f32[32,32,896]{2,0,1:T(8,128)S(1)} fusion(s32[64]{0:T(128)S(1)} %eq.48, bf16[8,8,32,896]{3,2,1,0:T(8,128)(2,1)} %bitcast.19), kind=kOutput, calls=%fused_computation.1 | convolution fusion | flops 117442560 | bytes 7340288 | tf_op jit(solution)/shard_map/dot_general | solution.py:404
  385.9 4.0 copy.35
  (12 shorter events, 0.1 us)
Async XLA Ops:
  8.0 216.2 %all-reduce.6.cloned.1.call-start = ((), (), s32[]{:S(2)}) async-start(), calls=%async_computation.1 | async-start | bytes 8257536
  10.3 1.5 copy-start
  77.9 1.9 copy-start.1
  132.3 0.7 copy-start.4
  231.6 150.0 %all-to-all-start = ((bf16[32,2,32,896]{3,2,1,0:T(8,128)(2,1)}), bf16[32,2,32,896]{3,2,1,0:T(8,128)(2,1)}, u32[]{:S(2)}, u32[]{:S(2)}) async-start(bf16[32,2,32,896]{3,2,1,0:T(8,128)(2,1)} %bitcast.31), calls=%async_computation | async-start | bytes 7340032 | tf_op jit(solution)/shard_map/all_to_all | solution.py:400
  239.3 0.7 copy-start.3
  239.3 136.1 %all-reduce.8.cloned.1.call-start = ((), (), s32[]{:S(2)}) async-start(), calls=%async_computation.2 | async-start | bytes 7340032 | tf_op jit(solution)/shard_map/psum | solution.py:410
  375.4 3.9 copy-start.2
Sparse Core Ops, SparseCore 0:
  132.4 91.7 all-reduce.5
Sparse Core Ops, SparseCore 1:
  244.3 131.1 all-reduce.7

commit v3 on v2

--- a/solution.py
+++ b/solution.py
@@ -40,8 +40,7 @@
     att_ref,
     gq_ref,
     part_ref,
-    gkw_ref,
-    gvw_ref,
+    gw_ref,
     gt_ref,
     weights,
     mixed_s,
@@ -134,10 +133,9 @@
 
         def one_head(h, carry):
             wide = pl.ds(pl.multiple_of(h * 2 * HD, 2 * HD), 2 * HD)
-            cols = pl.ds(pl.multiple_of(h * HD, HD), HD)
             term = jnp.dot(mixed_t[...], grads[:, wide], preferred_element_type=F32)
-            gkw_ref[:, cols] = term[:, :HD].astype(BF16)
-            gvw_ref[:, cols] = term[:, HD:].astype(BF16)
+            gw_ref[0, h] = term[:, :HD].astype(BF16)
+            gw_ref[1, h] = term[:, HD:].astype(BF16)
             return carry
 
         lax.fori_loop(0, heads, one_head, 0)
@@ -169,16 +167,14 @@
             span_rows,
             span_rows,
             blocks,
-            whole((ENC, width)),
-            whole((ENC, width)),
+            whole((2, heads, ENC, HD)),
             whole((KW, ENC)),
         ],
         out_shape=[
             jax.ShapeDtypeStruct((tokens, width), BF16),
             jax.ShapeDtypeStruct((tokens, width), BF16),
             jax.ShapeDtypeStruct(raw.shape, BF16),
-            jax.ShapeDtypeStruct((ENC, width), BF16),
-            jax.ShapeDtypeStruct((ENC, width), BF16),
+            jax.ShapeDtypeStruct((2, heads, ENC, HD), BF16),
             jax.ShapeDtypeStruct((KW, ENC), F32),
         ],
         scratch_shapes=[
@@ -362,6 +358,422 @@
     )(slots, table, states)
 
 
+def tail_kernel(
+    owners,
+    parts,
+    req_ref,
+    part_ref,
+    w_ref,
+    taps_ref,
+    back_ref,
+    wsum_ref,
+    tsum_ref,
+    from_far,
+    onward,
+    from_near,
+    send,
+    sibling_w,
+    pair_w,
+    first_in,
+    first_sum,
+    second_in,
+    taps_in,
+    taps_now,
+    far_send,
+    far_recv,
+    near_send,
+    near_recv,
+    back_send,
+    back_recv,
+    pair_send,
+    pair_recv,
+    axis_send,
+    axis_recv,
+    taps_send,
+    taps_recv,
+    *mine,
+):
+    me = lax.axis_index("dp")
+    y = lax.axis_index("db")
+    z, x, core = me // 8, lax.rem(me // 2, 4), lax.rem(me, 2)
+    sibling = me + 1 - 2 * core
+    right = lax.rem(y + 1, parts)
+    left = lax.rem(y + parts - 1, parts)
+    far = lax.rem(y + 2, parts)
+    requests = part_ref.shape[2]
+    half = requests // 2
+    capacity = 2
+    others = owners - 1
+    low, high = pl.ds(0, half), pl.ds(half, requests - half)
+
+    def x_peer(step):
+        return z * 8 + lax.rem(x + step, 4) * 2 + core
+
+    def z_peer(step):
+        return lax.rem(z + step, 4) * 8 + x * 2 + core
+
+    barrier = pltpu.get_barrier_semaphore()
+
+    def greet(step, carry):
+        pl.semaphore_signal(barrier, inc=1, device_id={"dp": dp_peer(step)})
+        return carry
+
+    lax.fori_loop(1, owners, greet, 0)
+    for other in range(1, parts):
+        pl.semaphore_signal(barrier, inc=1, device_id={"db": lax.rem(y + other, parts)})
+    pl.semaphore_wait(barrier, others + parts - 1)
+
+    def remote(src, dst, send_sem, recv_sem, where):
+        return pltpu.make_async_remote_copy(
+            src_ref=src, dst_ref=dst, send_sem=send_sem, recv_sem=recv_sem, device_id=where
+        )
+
+    def far_copy(side, c):
+        rows, to = ((low, right), (high, left))[side]
+        return remote(
+            part_ref.at[c, far, rows],
+            from_far.at[side, c],
+            far_send.at[side, c],
+            far_recv.at[side, c],
+            {"db": to},
+        )
+
+    def near_copy(side, c):
+        return remote(
+            onward.at[side, c],
+            from_near.at[side, c],
+            near_send.at[side, c],
+            near_recv.at[side, c],
+            {"db": (right, left)[side]},
+        )
+
+    def forward(c):
+        far_copy(0, c).wait_recv()
+        added = part_ref[c, right, 0:half].astype(F32) + from_far[0, c].astype(F32)
+        onward[0, c, 0:half] = added.astype(BF16)
+        onward[0, c, half:requests] = part_ref[c, right, half:requests]
+        near_copy(0, c).start()
+        far_copy(1, c).wait_recv()
+        added = part_ref[c, left, half:requests].astype(F32) + from_far[1, c].astype(F32)
+        onward[1, c, half:requests] = added.astype(BF16)
+        onward[1, c, 0:half] = part_ref[c, left, 0:half]
+        near_copy(1, c).start()
+
+    def give_back(c):
+        near_copy(0, c).wait_recv()
+        near_copy(1, c).wait_recv()
+        total = part_ref[c, y].astype(F32) + from_near[0, c].astype(F32)
+        mine[c][...] = (total + from_near[1, c].astype(F32)).astype(BF16)
+
+        def one(step, carry):
+            peer = dp_peer(step)
+            for k in range(capacity):
+                send[c, capacity * peer + k] = mine[c][req_ref[capacity * peer + k]]
+            remote(
+                send.at[c, pl.ds(capacity * peer, capacity)],
+                back_ref.at[c, pl.ds(capacity * me, capacity)],
+                back_send.at[c],
+                back_recv.at[c],
+                {"dp": peer},
+            ).start()
+            return carry
+
+        lax.fori_loop(1, owners, one, 0)
+        for k in range(capacity):
+            back_ref[c, capacity * me + k] = mine[c][req_ref[capacity * me + k]]
+
+    first_at, second_at = (x, z), (z, x)
+    first_peer, second_peer = (x_peer, z_peer), (z_peer, x_peer)
+    order = [(d, h) for d in (1, 2, 3, 0) for h in (0, 1)]
+
+    def group(h, step):
+        return h * 4 + lax.rem(first_at[h] + step, 4)
+
+    def pair_copy(d, h):
+        g = group(h, d)
+        return remote(
+            w_ref.at[1 - core, g],
+            sibling_w.at[g],
+            pair_send.at[0, h * 4 + d],
+            pair_recv.at[0, h * 4 + d],
+            {"dp": sibling},
+        )
+
+    def first_copy(d, h):
+        return remote(
+            pair_w.at[group(h, d)],
+            first_in.at[h, d - 1],
+            axis_send.at[0, h * 3 + d - 1],
+            axis_recv.at[0, h * 3 + d - 1],
+            {"dp": first_peer[h](d)},
+        )
+
+    def second_copy(d, h):
+        return remote(
+            first_sum.at[h, lax.rem(second_at[h] + d, 4)],
+            second_in.at[h, d - 1],
+            axis_send.at[1, h * 3 + d - 1],
+            axis_recv.at[1, h * 3 + d - 1],
+            {"dp": second_peer[h](d)},
+        )
+
+    def second_gather(d, h, back):
+        block = wsum_ref.at[core, group(h, 0), lax.rem(second_at[h] + back, 4)]
+        return remote(
+            block,
+            block,
+            axis_send.at[2, h * 3 + d - 1],
+            axis_recv.at[2, h * 3 + d - 1],
+            {"dp": second_peer[h](d)},
+        )
+
+    def first_gather(d, h, back):
+        block = wsum_ref.at[core, group(h, back)]
+        return remote(
+            block,
+            block,
+            axis_send.at[3, h * 3 + d - 1],
+            axis_recv.at[3, h * 3 + d - 1],
+            {"dp": first_peer[h](d)},
+        )
+
+    def pair_gather(d, h, which):
+        block = wsum_ref.at[which, group(h, 4 - d)]
+        return remote(
+            block,
+            block,
+            pair_send.at[1, h * 4 + d],
+            pair_recv.at[1, h * 4 + d],
+            {"dp": sibling},
+        )
+
+    def pair_sum(d, h):
+        pair_copy(d, h).wait_recv()
+        g = group(h, d)
+        pair_w[g] = (w_ref[core, g].astype(F32) + sibling_w[g].astype(F32)).astype(BF16)
+        if d:
+            first_copy(d, h).start()
+
+    def sum_first(h):
+        for d in (1, 2, 3):
+            first_copy(d, h).wait_recv()
+        total = pair_w[group(h, 0)].astype(F32)
+        for d in (1, 2, 3):
+            total = total + first_in[h, d - 1].astype(F32)
+        first_sum[h] = total.astype(BF16)
+        for d in (1, 2, 3):
+            second_copy(d, h).start()
+
+    def sum_second(h):
+        for d in (1, 2, 3):
+            second_copy(d, h).wait_recv()
+        total = first_sum[h, second_at[h]].astype(F32)
+        for d in (1, 2, 3):
+            total = total + second_in[h, d - 1].astype(F32)
+        wsum_ref[core, group(h, 0), second_at[h]] = total.astype(BF16)
+        for d in (1, 2, 3):
+            second_gather(d, h, 0).start()
+
+    def gather_first(h):
+        for d in (1, 2, 3):
+            second_gather(d, h, 4 - d).wait_recv()
+        for d in (1, 2, 3):
+            first_gather(d, h, 0).start()
+        pair_gather(0, h, core).start()
+
+    def gather_pair(h):
+        for d in (1, 2, 3):
+            first_gather(d, h, 4 - d).wait_recv()
+            pair_gather(d, h, core).start()
+
+    stages = (
+        (2, core, lambda step: {"dp": sibling}),
+        (4, x, lambda step: {"dp": x_peer(step)}),
+        (4, z, lambda step: {"dp": z_peer(step)}),
+        (parts, y, lambda step: {"db": lax.rem(y + step, parts)}),
+    )
+
+    def taps_copy(stage, d):
+        count, at, peer = stages[stage]
+        return remote(
+            taps_now.at[stage],
+            taps_in.at[stage, at],
+            taps_send.at[stage, d - 1],
+            taps_recv.at[stage, d - 1],
+            peer(d),
+        )
+
+    def taps_start(stage, value):
+        count, at, peer = stages[stage]
+        taps_now[stage] = value
+        taps_in[stage, at] = value
+        for d in range(1, count):
+            taps_copy(stage, d).start()
+
+    def taps_end(stage):
+        count = stages[stage][0]
+        for d in range(1, count):
+            taps_copy(stage, d).wait_recv()
+        total = taps_in[stage, 0]
+        for other in range(1, count):
+            total = total + taps_in[stage, other]
+        return total
+
+    for d, h in order[:2]:
+        pair_copy(d, h).start()
+    for c in range(CHUNKS):
+        far_copy(0, c).start()
+        far_copy(1, c).start()
+    for d, h in order[2:]:
+        pair_copy(d, h).start()
+    taps_start(0, taps_ref[...])
+    for i in range(8):
+        pair_sum(*order[i])
+        if i < CHUNKS:
+            forward(i)
+    taps_start(1, taps_end(0))
+    for c in range(CHUNKS):
+        give_back(c)
+        if c == 1:
+            sum_first(0)
+            sum_first(1)
+            taps_start(2, taps_end(1))
+        if c == 3:
+            sum_second(0)
+            sum_second(1)
+            taps_start(3, taps_end(2))
+        if c == 4:
+            gather_first(0)
+            gather_first(1)
+    gather_pair(0)
+    gather_pair(1)
+    tsum_ref[...] = taps_end(3)
+
+    for d, h in order:
+        pair_gather(d, h, 1 - core).wait_recv()
+        pair_gather(d, h, core).wait_send()
+        pair_copy(d, h).wait_send()
+        if d:
+            first_copy(d, h).wait_send()
+            second_copy(d, h).wait_send()
+            second_gather(d, h, 0).wait_send()
+            first_gather(d, h, 0).wait_send()
+    for stage in range(4):
+        for d in range(1, stages[stage][0]):
+            taps_copy(stage, d).wait_send()
+    for c in range(CHUNKS):
+        for side in (0, 1):
+            far_copy(side, c).wait_send()
+            near_copy(side, c).wait_send()
+        most = send.at[c, pl.ds(0, capacity * others)]
+        pltpu.make_async_copy(most, most, back_send.at[c]).wait()
+        most = back_ref.at[c, pl.ds(0, capacity * others)]
+        pltpu.make_async_copy(most, most, back_recv.at[c]).wait()
+
+
+def tail(wanted, part, weights, taps):
+    owners = lax.axis_size("dp")
+    parts = lax.axis_size("db")
+    requests, quarter = part.shape[2], part.shape[3]
+    slots = wanted.shape[0]
+    vmem = pl.BlockSpec(memory_space=pltpu.VMEM)
+    dma = pltpu.SemaphoreType.DMA
+    heads = weights.shape[1]
+    rows = ENC // 4
+    weights = weights.reshape(2, heads, 4, rows, HD)
+    both = (2, CHUNKS, requests, quarter, LANES)
+    return pl.pallas_call(
+        functools.partial(tail_kernel, owners, parts),
+        in_specs=[pl.BlockSpec(memory_space=pltpu.SMEM), vmem, vmem, vmem],
+        out_specs=[vmem, vmem, vmem],
+        out_shape=[
+            jax.ShapeDtypeStruct((CHUNKS, slots, quarter, LANES), BF16),
+            jax.ShapeDtypeStruct(weights.shape, BF16),
+            jax.ShapeDtypeStruct(taps.shape, F32),
+        ],
+        scratch_shapes=[
+            pltpu.VMEM((2, CHUNKS, requests // 2, quarter, LANES), BF16),
+            pltpu.VMEM(both, BF16),
+            pltpu.VMEM(both, BF16),
+            pltpu.VMEM((CHUNKS, slots, quarter, LANES), BF16),
+            pltpu.VMEM((heads, 4, rows, HD), BF16),
+            pltpu.VMEM((heads, 4, rows, HD), BF16),
+            pltpu.VMEM((2, 3, 4, rows, HD), BF16),
+            pltpu.VMEM((2, 4, rows, HD), BF16),
+            pltpu.VMEM((2, 3, rows, HD), BF16),
+            pltpu.VMEM((4, 4) + taps.shape, F32),
+            pltpu.VMEM((4,) + taps.shape, F32),
+            dma((2, CHUNKS)),
+            dma((2, CHUNKS)),
+            dma((2, CHUNKS)),
+            dma((2, CHUNKS)),
+            dma((CHUNKS,)),
+            dma((CHUNKS,)),
+            dma((2, 8)),
+            dma((2, 8)),
+            dma((4, 6)),
+            dma((4, 6)),
+            dma((4, 3)),
+            dma((4, 3)),
+        ]
+        + [pltpu.VMEM((requests, quarter, LANES), BF16)] * CHUNKS,
+        compiler_params=pltpu.CompilerParams(
+            collective_id=1, has_side_effects=True, vmem_limit_bytes=48 * 1024 * 1024
+        ),
+        cost_estimate=pl.CostEstimate(flops=0, bytes_accessed=30_000_000, transcendentals=0),
+    )(wanted, part, weights, taps)
+
+
+def spread_kernel(rows_ref, back_ref, w_ref, states_ref, gkw_ref, gvw_ref):
+    gkw_ref[...] = w_ref[0, 0].astype(F32)
+    gvw_ref[...] = w_ref[1, 0].astype(F32)
+
+    @pl.when(pl.program_id(0) < CHUNKS)
+    def _():
+        states_ref[...] = jnp.zeros_like(states_ref)
+
+        def add(slot, carry):
+            row = rows_ref[slot]
+
+            @pl.when(row >= 0)
+            def _():
+                states_ref[row] += back_ref[0, slot].astype(F32)
+
+            return carry
+
+        lax.fori_loop(0, rows_ref.shape[0], add, 0)
+
+
+def spread(rows, back, weights, blocks):
+    heads = weights.shape[1]
+    slots, quarter = back.shape[1], back.shape[2]
+    last = CHUNKS - 1
+    head_cols = pl.BlockSpec((ENC, HD), lambda i: (0, i))
+    return pl.pallas_call(
+        spread_kernel,
+        grid=(max(heads, CHUNKS),),
+        in_specs=[
+            pl.BlockSpec(memory_space=pltpu.SMEM),
+            pl.BlockSpec((1, slots, quarter, LANES), lambda i: (jnp.minimum(i, last), 0, 0, 0)),
+            pl.BlockSpec((2, 1, ENC, HD), lambda i: (0, i, 0, 0)),
+        ],
+        out_specs=[
+            pl.BlockSpec((blocks, quarter, LANES), lambda i: (0, 0, jnp.minimum(i, last))),
+            head_cols,
+            head_cols,
+        ],
+        out_shape=[
+            jax.ShapeDtypeStruct((blocks, quarter, ENC), F32),
+            jax.ShapeDtypeStruct((ENC, heads * HD), F32),
+            jax.ShapeDtypeStruct((ENC, heads * HD), F32),
+        ],
+        compiler_params=pltpu.CompilerParams(
+            dimension_semantics=("arbitrary",), vmem_limit_bytes=32 * 1024 * 1024
+        ),
+        cost_estimate=pl.CostEstimate(flops=0, bytes_accessed=19_000_000, transcendentals=0),
+    )(rows, back, weights.reshape(2, heads, ENC, HD))
+
+
 def shards(
     queries, cotangent, db_states, key_weight, value_weight, conv_kernel, nbr_owner, nbr_row
 ):
@@ -383,39 +795,25 @@
     used_slot = jnp.any(slot_hits, axis=0)
     row_sent = jnp.sum(jnp.where(slot_hits, row_flat[:, None], 0), axis=0)
     row_table = jnp.where(used_slot, row_sent, -1).reshape(owners, capacity)
-    slot_matrix = slot_hits.astype(jnp.bfloat16)
+    wanted = jnp.sum(jnp.where(slot_hits, positions[:, None], 0), axis=0)
     table = jnp.pad(row_table[:, None, :], ((0, 0), (0, 0), (0, LANES - capacity)))
     raw, asked = fetch(target, table, db_states)
     asked_flat = asked[:, 0, :capacity].reshape(slots_total)
-    attended, grad_query, part, key_term, value_term, taps_term = core(
+    attended, grad_query, part, weight_terms, taps_term = core(
         queries, cotangent, raw, key_weight, value_weight, conv_kernel
     )
-    grad_raw = lax.psum_scatter(part, "db", scatter_dimension=1, tiled=True)
-    grad_raw = jnp.transpose(grad_raw.reshape(CHUNKS, request_count, quarter, LANES), (1, 2, 0, 3))
-    grad_raw_b = grad_raw.reshape(request_count, quarter * ENC)
-    grad_send = jnp.einsum(
-        "ns,nf->sf", slot_matrix, grad_raw_b, preferred_element_type=jnp.float32
-    ).astype(jnp.bfloat16)
-    grad_send = grad_send.reshape(owners, capacity, quarter, ENC)
-    grad_back = lax.all_to_all(grad_send, "dp", split_axis=0, concat_axis=0, tiled=True)
-    picker_back = (
-        jnp.arange(local_blocks, dtype=jnp.int32)[:, None] == asked_flat[None, :]
-    ).astype(jnp.bfloat16)
-    grad_states = jnp.dot(
-        picker_back,
-        grad_back.reshape(slots_total, quarter * ENC),
-        preferred_element_type=jnp.float32,
+    taps_term = jnp.pad(taps_term, ((0, 8 - KW), (0, 0)))
+    back, weight_sums, taps_sum = tail(wanted, part, weight_terms, taps_term)
+    grad_states, grad_key_weight, grad_value_weight = spread(
+        asked_flat, back, weight_sums, local_blocks
     )
-    grad_states = grad_states.reshape(local_blocks, quarter, ENC)
-    grad_key_weight, grad_value_weight = lax.psum((key_term, value_term), "dp")
-    grad_kernel = lax.psum(taps_term, ("dp", "db"))
     return (
         attended,
         grad_query,
         grad_states,
-        grad_key_weight.astype(F32),
-        grad_value_weight.astype(F32),
-        grad_kernel,
+        grad_key_weight,
+        grad_value_weight,
+        taps_sum[:KW],
     )
 
 

time: 398 us -> 227 us (0.57)
  waiting for transfers between devices: 122 us -> 0 us
  blocking collectives: 105 us -> 0 us
  Pallas kernels: 119 us -> 217 us
  between operations: 15.6 us -> 0.7 us
  local copies, waits for them, and re-layouts: 16.7 us -> 8.74 us
  starting transfers between devices: 7.8 us -> 0 us
  other arithmetic: 6.51 us -> 0.38 us
  matrix products: 5.56 us -> 0 us
    psum x1 -> x0, blocking collectives: 105 us -> none  [shards(): grad_kernel = lax.psum(taps_term, ('dp', 'db'))]
    pallas_call x0 -> x2, Pallas kernels: none -> 98.3 us  [the longest x1 89 us: tail(): pl.pallas_call(functools.partial(tail_kernel, owners, parts), in_specs=[p...]
    unnamed x3 -> x0, waiting for transfers between devices: 91.2 us -> none
    psum x1 -> x0, waiting for transfers between devices: 30.8 us -> none  [shards(): grad_key_weight, grad_value_weight = lax.psum((key_term, value_term), 'dp')]
    all_to_all x1 -> x0, starting transfers between devices: 7.72 us -> none  [shards(): lax.all_to_all(grad_send, 'dp', split_axis=0, concat_axis=0, tiled=True)]
    convert_element_type x2 -> x0, other arithmetic: 6.13 us -> none  [the longest x1 3.88 us: shards(): grad_key_weight.astype(F32)]
    unnamed x15 -> x8, local copies, waits for them, and re-layouts: 12.6 us -> 7 us
    dot_general x2 -> x0, matrix products: 5.56 us -> none  [the longest x1 4.34 us: shards(): jnp.dot(picker_back, grad_back.reshape(slots_total, quarter * ENC), prefe...]
  transfers between devices with their start and end apart: 3 -> 0, of which waited for: 2 -> 0; matrix products, arithmetic and copies ran while one was open for 2% -> 0% of each run, Pallas kernels for 0% -> 0%
where the time goes in v3:
time: 227 us
  Pallas kernels  217 us (96%)
  local copies, waits for them, and re-layouts  8.74 us (4%)
    pallas_call x1, Pallas kernels, tail(): pl.pallas_call(functools.partial(tail_kernel, owners, parts), in_specs=[p...  89 us
    pallas_call x1, Pallas kernels, fetch(): pl.pallas_call(functools.partial(fetch_kernel, owners, parts), in_specs=[...  66.1 us
    pallas_call x1, Pallas kernels, core(): pl.pallas_call(functools.partial(core_kernel, heads), grid=(spans,), in_s...  52.5 us
    pallas_call x1, Pallas kernels, spread(): pl.pallas_call(spread_kernel, grid=(max(heads, CHUNKS),), in_specs=[pl.Bl...  9.31 us
    unnamed x8, local copies, waits for them, and re-layouts  7 us

profile of v3, /device:TPU:1, one launch (start us, length us, event | category | flops | bytes accessed | tf_op | source)
XLA Modules:
  0.0 226.7 jit_solution(459079138481780559)
XLA Ops:
  0.6 0.8 copy.20
  1.4 0.1 reshape.51
  1.5 0.2 convert_reduce_fusion
  1.7 0.1 fusion
  1.8 0.8 copy.21
  2.5 0.1 broadcast_in_dim.29
  2.6 0.1 select_reduce_fusion
  2.7 0.1 select_n.23
  2.9 0.0 copy-start.1
  2.9 1.5 copy-done.1
  4.4 66.1 %shard_map.127 = (bf16[7,4,18,32,128]{4,3,2,1,0:T(8,128)(2,1)S(1)}, s32[32,1,128]{2,1,0:T(1,128)S(1)}) custom-call(s32[18]{0:T(128)S(1)} %multiply_add_fusion.slot_ref, s32[32,1,128]{2,1,0:T(1,128)S(1)} %pad.8.table_ref, bf16[32,32,896]{2,1,0:T(8,128)(2,1)S(1)} %copy-done.1), custom_call_target="tpu_custom_call" | custom-call | bytes 16000000 | tf_op jit(solution)/shard_map/pallas_call | solution.py:335
  70.5 0.0 copy-start.2
  70.5 1.9 copy-done.2
  72.5 0.1 reshape_squeeze.3.rows_ref
  72.6 52.5 %shard_map.128 = (bf16[576,1024]{1,0:T(8,128)(2,1)}, bf16[576,1024]{1,0:T(8,128)(2,1)}, bf16[7,4,18,32,128]{4,3,2,1,0:T(8,128)(2,1)}, bf16[2,8,896,128]{3,2,1,0:T(8,128)(2,1)}, f32[3,896]{1,0:T(4,128)}) custom-call(bf16[576,1024]{1,0:T(8,128)(2,1)} %q_ref.1, bf16[576,1024]{1,0:T(8,128)(2,1)} %g_ref.1, bf16[7,4,18,32,128]{4,3,2,1,0:T(8,128)(2,1)} %copy-done.2, ...), custom_call_target="tpu_custom_call" | custom-call | flops 27000000512 | bytes 30000000 | tf_op jit(solution)/shard_map/pallas_call | solution.py:155
  125.0 0.7 pad.9.taps_ref
  125.8 89.0 %shard_map.129 = (bf16[7,64,32,128]{3,2,1,0:T(8,128)(2,1)S(1)}, bf16[2,8,4,224,128]{4,3,2,1,0:T(8,128)(2,1)}, f32[8,896]{1,0:T(8,128)S(1)}) custom-call(s32[64]{0:T(128)S(1)} %get-tuple-element.32.req_ref, bf16[7,4,18,32,128]{4,3,2,1,0:T(8,128)(2,1)} %get-tuple-element.23.part_ref, bf16[2,8,4,224,128]{4,3,2,1,0:T(8,128)(2,1)} %bitcast.4, ...), custom_call_target="tpu_custom_call" | custom-call | bytes 30000000 | tf_op jit(solution)/shard_map/pallas_call | solution.py:685
  214.8 0.6 slice.7
  215.4 0.0 copy-start
  215.4 2.0 copy-done
  217.4 9.3 %shard_map.130 = (f32[32,32,896]{2,1,0:T(8,128)}, f32[896,1024]{1,0:T(8,128)}, f32[896,1024]{1,0:T(8,128)}) custom-call(s32[64]{0:T(128)S(1)} %reshape_squeeze.3.rows_ref, bf16[7,64,32,128]{3,2,1,0:T(8,128)(2,1)S(1)} %get-tuple-element.26.back_ref, bf16[2,8,896,128]{3,2,1,0:T(8,128)(2,1)S(1)} %bitcast.3), custom_call_target="tpu_custom_call" | custom-call | bytes 19000000 | tf_op jit(solution)/shard_map/pallas_call | solution.py:752
  (4 shorter events, 0.1 us)
Async XLA Ops:
  2.9 1.5 copy-start.1
  70.5 1.9 copy-start.2
  215.4 2.0 copy-start

commit v4 on v3

--- a/solution.py
+++ b/solution.py
@@ -39,30 +39,14 @@
     taps_ref,
     att_ref,
     gq_ref,
-    part_ref,
-    gw_ref,
-    gt_ref,
-    weights,
+    grads_ref,
+    mixed_ref,
     mixed_s,
-    mixed_t,
-    grads,
-    gm_s,
-    taps_acc,
     kv_s,
     both_s,
     stacked_s,
 ):
-    span = pl.program_id(0)
     scale = 1.0 / math.sqrt(HD)
-    keys_here = NBR * NLEN
-
-    @pl.when(span == 0)
-    def _():
-        for h in range(heads):
-            weights[:, 2 * h * HD : (2 * h + 1) * HD] = kw_ref[:, h * HD : (h + 1) * HD]
-            weights[:, (2 * h + 1) * HD : (2 * h + 2) * HD] = vw_ref[:, h * HD : (h + 1) * HD]
-        taps_acc[...] = jnp.zeros_like(taps_acc)
-
     for c in range(CHUNKS):
         cols = slice(c * LANES, (c + 1) * LANES)
         for n in range(NBR):
@@ -73,11 +57,14 @@
             mixed = mixed + taps_ref[2:3, cols] * up
             mixed_s[n * NLEN : (n + 1) * NLEN, cols] = mixed.astype(BF16)
     mixed = mixed_s[...]
-    rows = pl.ds(pl.multiple_of(span * keys_here, keys_here), keys_here)
-    mixed_t[:, rows] = mixed.T
+    mixed_ref[...] = mixed.T
 
     zeros = jnp.zeros((SPAN, HD), BF16)
-    kv_s[...] = jnp.dot(mixed, weights[...], preferred_element_type=F32).astype(BF16)
+    for place, weight in enumerate((kw_ref, vw_ref)):
+        states = jnp.dot(mixed, weight[...], preferred_element_type=F32).astype(BF16)
+        for h in range(heads):
+            at = (2 * h + place) * HD
+            kv_s[:, at : at + HD] = states[:, h * HD : (h + 1) * HD]
 
     def diag(h):
         q = q_ref[:, h * HD : (h + 1) * HD]
@@ -105,47 +92,20 @@
         gq_ref[:, cols] = out[:SPAN, :HD].astype(BF16)
         att_ref[:, cols] = out[SPAN:, HD:].astype(BF16)
     for h in range(heads):
-        wide = slice(2 * h * HD, (2 * h + 2) * HD)
-        grads[rows, wide] = lax.dot_general(
+        cols = slice(h * HD, (h + 1) * HD)
+        pair = lax.dot_general(
             stacked_s[h], diag(h), (((0,), (0,)), ((), ())), preferred_element_type=F32
         ).astype(BF16)
-
-    gm_s[...] = lax.dot_general(grads[rows, :], weights[...], NT, preferred_element_type=F32)
-    for c in range(CHUNKS):
-        cols = slice(c * LANES, (c + 1) * LANES)
-        for n in range(NBR):
-            gm = gm_s[n * NLEN : (n + 1) * NLEN, cols]
-            gm_down, gm_up = shifted(gm)
-            back = taps_ref[0:1, cols] * gm_up
-            back = back + taps_ref[1:2, cols] * gm
-            back = back + taps_ref[2:3, cols] * gm_down
-            part_ref[c, :, n] = back.astype(BF16).reshape(part_ref.shape[1], -1, LANES)
-            raw = raw_ref[c, :, n].reshape(NLEN, LANES).astype(F32)
-            down, up = shifted(raw)
-            for w, other in enumerate((down, raw, up)):
-                taps_acc[w, :, cols] += jnp.sum(
-                    (gm * other).reshape(NLEN // 8, 8, LANES), axis=0
-                )
-
-    @pl.when(span == pl.num_programs(0) - 1)
-    def _():
-        gt_ref[...] = jnp.sum(taps_acc[...], axis=1)
-
-        def one_head(h, carry):
-            wide = pl.ds(pl.multiple_of(h * 2 * HD, 2 * HD), 2 * HD)
-            term = jnp.dot(mixed_t[...], grads[:, wide], preferred_element_type=F32)
-            gw_ref[0, h] = term[:, :HD].astype(BF16)
-            gw_ref[1, h] = term[:, HD:].astype(BF16)
-            return carry
-
-        lax.fori_loop(0, heads, one_head, 0)
+        grads_ref[0, :, cols] = pair[:, :HD]
+        grads_ref[1, :, cols] = pair[:, HD:]
 
 
 def core(queries, cotangent, raw, key_weight, value_weight, conv_kernel):
     tokens, width = queries.shape
     heads = width // HD
     spans = tokens // SPAN
-    keys_all = spans * NBR * NLEN
+    keys_here = NBR * NLEN
+    keys_all = spans * keys_here
     whole = lambda shape: pl.BlockSpec(
         shape, lambda i: (0,) * len(shape), pipeline_mode=pl.Buffered(1)
     )
@@ -166,33 +126,26 @@
         out_specs=[
             span_rows,
             span_rows,
-            blocks,
-            whole((2, heads, ENC, HD)),
-            whole((KW, ENC)),
+            pl.BlockSpec((2, keys_here, width), lambda i: (0, i, 0)),
+            pl.BlockSpec((ENC, keys_here), lambda i: (0, i)),
         ],
         out_shape=[
             jax.ShapeDtypeStruct((tokens, width), BF16),
             jax.ShapeDtypeStruct((tokens, width), BF16),
-            jax.ShapeDtypeStruct(raw.shape, BF16),
-            jax.ShapeDtypeStruct((2, heads, ENC, HD), BF16),
-            jax.ShapeDtypeStruct((KW, ENC), F32),
+            jax.ShapeDtypeStruct((2, keys_all, width), BF16),
+            jax.ShapeDtypeStruct((ENC, keys_all), BF16),
         ],
         scratch_shapes=[
-            pltpu.VMEM((ENC, 2 * width), BF16),
-            pltpu.VMEM((NBR * NLEN, ENC), BF16),
-            pltpu.VMEM((ENC, keys_all), BF16),
-            pltpu.VMEM((keys_all, 2 * width), BF16),
-            pltpu.VMEM((NBR * NLEN, ENC), F32),
-            pltpu.VMEM((KW, 8, ENC), F32),
-            pltpu.VMEM((NBR * NLEN, 2 * width), BF16),
-            pltpu.VMEM((heads, 2 * SPAN, NBR * NLEN), F32),
-            pltpu.VMEM((heads, 2 * SPAN, NBR * NLEN), BF16),
+            pltpu.VMEM((keys_here, ENC), BF16),
+            pltpu.VMEM((keys_here, 2 * width), BF16),
+            pltpu.VMEM((heads, 2 * SPAN, keys_here), F32),
+            pltpu.VMEM((heads, 2 * SPAN, keys_here), BF16),
         ],
         compiler_params=pltpu.CompilerParams(
-            dimension_semantics=("arbitrary",), vmem_limit_bytes=56 * 1024 * 1024
+            dimension_semantics=("arbitrary",), vmem_limit_bytes=40 * 1024 * 1024
         ),
         cost_estimate=pl.CostEstimate(
-            flops=27_000_000_000, bytes_accessed=30_000_000, transcendentals=1_200_000
+            flops=10_000_000_000, bytes_accessed=30_000_000, transcendentals=1_200_000
         ),
     )(queries, cotangent, raw, key_weight, value_weight, conv_kernel)
 
@@ -362,12 +315,25 @@
     owners,
     parts,
     req_ref,
-    part_ref,
-    w_ref,
-    taps_ref,
+    conv_ref,
+    grads_hbm,
+    mixed_hbm,
+    raw_hbm,
+    kw_hbm,
+    vw_hbm,
     back_ref,
     wsum_ref,
     tsum_ref,
+    grads,
+    mixed_t,
+    raw_ref,
+    kw_ref,
+    vw_ref,
+    part_ref,
+    w_ref,
+    taps_acc,
+    load_sem,
+    grads_sem,
     from_far,
     onward,
     from_near,
@@ -401,6 +367,27 @@
     left = lax.rem(y + parts - 1, parts)
     far = lax.rem(y + 2, parts)
     requests = part_ref.shape[2]
+    keys_here = NBR * NLEN
+    spans = requests // NBR
+
+    def load(index):
+        pair = ((kw_hbm, kw_ref), (vw_hbm, vw_ref), (raw_hbm, raw_ref), (mixed_hbm, mixed_t))[index]
+        return pltpu.make_async_copy(*pair, load_sem.at[index])
+
+    def load_grads(span):
+        rows = pl.ds(pl.multiple_of(span * keys_here, keys_here), keys_here)
+        return pltpu.make_async_copy(
+            grads_hbm.at[:, rows], grads.at[:, rows], grads_sem.at[span]
+        )
+
+    load(0).start()
+    load(1).start()
+    load_grads(0).start()
+    load(2).start()
+    for span in range(1, spans):
+        load_grads(span).start()
+    load(3).start()
+    taps_acc[...] = jnp.zeros_like(taps_acc)
     half = requests // 2
     capacity = 2
     others = owners - 1
@@ -427,6 +414,41 @@
         return pltpu.make_async_remote_copy(
             src_ref=src, dst_ref=dst, send_sem=send_sem, recv_sem=recv_sem, device_id=where
         )
+
+    def grad_columns(chunks, first):
+        cols = slice(chunks[0] * LANES, (chunks[-1] + 1) * LANES)
+
+        def one(span, carry):
+            if first:
+                load_grads(span).wait()
+            rows = pl.ds(pl.multiple_of(span * keys_here, keys_here), keys_here)
+            whole = lax.dot_general(
+                grads[0, rows], kw_ref[cols], NT, preferred_element_type=F32
+            ) + lax.dot_general(grads[1, rows], vw_ref[cols], NT, preferred_element_type=F32)
+            for i, c in enumerate(chunks):
+                lanes = slice(c * LANES, (c + 1) * LANES)
+                for n in range(NBR):
+                    gm = whole[n * NLEN : (n + 1) * NLEN, i * LANES : (i + 1) * LANES]
+                    gm_down, gm_up = shifted(gm)
+                    grad = conv_ref[0:1, lanes] * gm_up
+                    grad = grad + conv_ref[1:2, lanes] * gm
+                    grad = grad + conv_ref[2:3, lanes] * gm_down
+                    part_ref[c, :, span * NBR + n] = grad.astype(BF16).reshape(parts, -1, LANES)
+                    raw = raw_ref[c, :, span * NBR + n].reshape(NLEN, LANES).astype(F32)
+                    for w, other in enumerate((gm_up, gm, gm_down)):
+                        taps_acc[w, :, lanes] += jnp.sum(
+                            (raw * other).reshape(NLEN // 8, 8, LANES), axis=0
+                        )
+            return carry
+
+        lax.fori_loop(0, spans, one, 0)
+
+    def weight_terms(which, pair):
+        wide = pl.ds(pair * 2 * HD, 2 * HD)
+        term = jnp.dot(mixed_t[...], grads[which, :, wide], preferred_element_type=F32)
+        for i in (0, 1):
+            block = term[:, i * HD : (i + 1) * HD].astype(BF16)
+            w_ref[which, 2 * pair + i] = block.reshape(4, -1, HD)
 
     def far_copy(side, c):
         rows, to = ((low, right), (high, left))[side]
@@ -489,13 +511,12 @@
     def group(h, step):
         return h * 4 + lax.rem(first_at[h] + step, 4)
 
-    def pair_copy(d, h):
-        g = group(h, d)
+    def pair_copy(g):
         return remote(
             w_ref.at[1 - core, g],
             sibling_w.at[g],
-            pair_send.at[0, h * 4 + d],
-            pair_recv.at[0, h * 4 + d],
+            pair_send.at[0, g],
+            pair_recv.at[0, g],
             {"dp": sibling},
         )
 
@@ -548,7 +569,6 @@
         )
 
     def pair_sum(d, h):
-        pair_copy(d, h).wait_recv()
         g = group(h, d)
         pair_w[g] = (w_ref[core, g].astype(F32) + sibling_w[g].astype(F32)).astype(BF16)
         if d:
@@ -619,32 +639,59 @@
             total = total + taps_in[stage, other]
         return total
 
-    for d, h in order[:2]:
-        pair_copy(d, h).start()
-    for c in range(CHUNKS):
+    load(0).wait()
+    load(1).wait()
+    load(2).wait()
+    grad_columns((0, 1), True)
+    for c in (0, 1):
         far_copy(0, c).start()
         far_copy(1, c).start()
-    for d, h in order[2:]:
-        pair_copy(d, h).start()
-    taps_start(0, taps_ref[...])
-    for i in range(8):
-        pair_sum(*order[i])
-        if i < CHUNKS:
-            forward(i)
+    load(3).wait()
+    for pair in range(4):
+        weight_terms(1 - core, pair)
+        pair_copy(2 * pair).start()
+        pair_copy(2 * pair + 1).start()
+        if pair in (1, 2):
+            forward(pair - 1)
+    for pair in range(4):
+        weight_terms(core, pair)
+        if pair in (1, 3):
+            give_back(pair // 2)
+    for g in range(8):
+        pair_copy(g).wait_recv()
+    for d, h in order:
+        pair_sum(d, h)
+    grad_columns((2, 3), False)
+    for c in (2, 3):
+        far_copy(0, c).start()
+        far_copy(1, c).start()
+    grad_columns((4, 5), False)
+    for c in (4, 5):
+        far_copy(0, c).start()
+        far_copy(1, c).start()
+    forward(2)
+    forward(3)
+    sum_first(0)
+    sum_first(1)
+    grad_columns((6,), False)
+    far_copy(0, 6).start()
+    far_copy(1, 6).start()
+    taps_start(0, jnp.sum(taps_acc[...], axis=1))
+    give_back(2)
+    forward(4)
+    forward(5)
+    sum_second(0)
+    sum_second(1)
+    give_back(3)
+    forward(6)
     taps_start(1, taps_end(0))
-    for c in range(CHUNKS):
-        give_back(c)
-        if c == 1:
-            sum_first(0)
-            sum_first(1)
-            taps_start(2, taps_end(1))
-        if c == 3:
-            sum_second(0)
-            sum_second(1)
-            taps_start(3, taps_end(2))
-        if c == 4:
-            gather_first(0)
-            gather_first(1)
+    gather_first(0)
+    gather_first(1)
+    give_back(4)
+    taps_start(2, taps_end(1))
+    give_back(5)
+    taps_start(3, taps_end(2))
+    give_back(6)
     gather_pair(0)
     gather_pair(1)
     tsum_ref[...] = taps_end(3)
@@ -652,7 +699,7 @@
     for d, h in order:
         pair_gather(d, h, 1 - core).wait_recv()
         pair_gather(d, h, core).wait_send()
-        pair_copy(d, h).wait_send()
+        pair_copy(h * 4 + d).wait_send()
         if d:
             first_copy(d, h).wait_send()
             second_copy(d, h).wait_send()
@@ -671,27 +718,39 @@
         pltpu.make_async_copy(most, most, back_recv.at[c]).wait()
 
 
-def tail(wanted, part, weights, taps):
+def tail(wanted, conv_kernel, grads, mixed, raw, key_weight, value_weight):
     owners = lax.axis_size("dp")
     parts = lax.axis_size("db")
-    requests, quarter = part.shape[2], part.shape[3]
+    requests, quarter = raw.shape[2], raw.shape[3]
     slots = wanted.shape[0]
     vmem = pl.BlockSpec(memory_space=pltpu.VMEM)
+    anywhere = pl.BlockSpec(memory_space=pl.ANY)
     dma = pltpu.SemaphoreType.DMA
-    heads = weights.shape[1]
+    heads = key_weight.shape[1] // HD
     rows = ENC // 4
-    weights = weights.reshape(2, heads, 4, rows, HD)
+    weights = (2, heads, 4, rows, HD)
+    taps = (8, ENC)
     both = (2, CHUNKS, requests, quarter, LANES)
     return pl.pallas_call(
         functools.partial(tail_kernel, owners, parts),
-        in_specs=[pl.BlockSpec(memory_space=pltpu.SMEM), vmem, vmem, vmem],
+        in_specs=[pl.BlockSpec(memory_space=pltpu.SMEM), vmem] + [anywhere] * 5,
         out_specs=[vmem, vmem, vmem],
         out_shape=[
             jax.ShapeDtypeStruct((CHUNKS, slots, quarter, LANES), BF16),
-            jax.ShapeDtypeStruct(weights.shape, BF16),
-            jax.ShapeDtypeStruct(taps.shape, F32),
+            jax.ShapeDtypeStruct(weights, BF16),
+            jax.ShapeDtypeStruct(taps, F32),
         ],
         scratch_shapes=[
+            pltpu.VMEM(grads.shape, BF16),
+            pltpu.VMEM(mixed.shape, BF16),
+            pltpu.VMEM(raw.shape, BF16),
+            pltpu.VMEM(key_weight.shape, BF16),
+            pltpu.VMEM(value_weight.shape, BF16),
+            pltpu.VMEM(raw.shape, BF16),
+            pltpu.VMEM(weights, BF16),
+            pltpu.VMEM((8, 8, ENC), F32),
+            dma((4,)),
+            dma((requests // NBR,)),
             pltpu.VMEM((2, CHUNKS, requests // 2, quarter, LANES), BF16),
             pltpu.VMEM(both, BF16),
             pltpu.VMEM(both, BF16),
@@ -701,8 +760,8 @@
             pltpu.VMEM((2, 3, 4, rows, HD), BF16),
             pltpu.VMEM((2, 4, rows, HD), BF16),
             pltpu.VMEM((2, 3, rows, HD), BF16),
-            pltpu.VMEM((4, 4) + taps.shape, F32),
-            pltpu.VMEM((4,) + taps.shape, F32),
+            pltpu.VMEM((4, 4) + taps, F32),
+            pltpu.VMEM((4,) + taps, F32),
             dma((2, CHUNKS)),
             dma((2, CHUNKS)),
             dma((2, CHUNKS)),
@@ -718,10 +777,12 @@
         ]
         + [pltpu.VMEM((requests, quarter, LANES), BF16)] * CHUNKS,
         compiler_params=pltpu.CompilerParams(
-            collective_id=1, has_side_effects=True, vmem_limit_bytes=48 * 1024 * 1024
+            collective_id=1, has_side_effects=True, vmem_limit_bytes=60 * 1024 * 1024
         ),
-        cost_estimate=pl.CostEstimate(flops=0, bytes_accessed=30_000_000, transcendentals=0),
-    )(wanted, part, weights, taps)
+        cost_estimate=pl.CostEstimate(
+            flops=17_000_000_000, bytes_accessed=30_000_000, transcendentals=0
+        ),
+    )(wanted, conv_kernel, grads, mixed, raw, key_weight, value_weight)
 
 
 def spread_kernel(rows_ref, back_ref, w_ref, states_ref, gkw_ref, gvw_ref):
@@ -799,11 +860,12 @@
     table = jnp.pad(row_table[:, None, :], ((0, 0), (0, 0), (0, LANES - capacity)))
     raw, asked = fetch(target, table, db_states)
     asked_flat = asked[:, 0, :capacity].reshape(slots_total)
-    attended, grad_query, part, weight_terms, taps_term = core(
+    attended, grad_query, grads, mixed = core(
         queries, cotangent, raw, key_weight, value_weight, conv_kernel
     )
-    taps_term = jnp.pad(taps_term, ((0, 8 - KW), (0, 0)))
-    back, weight_sums, taps_sum = tail(wanted, part, weight_terms, taps_term)
+    back, weight_sums, taps_sum = tail(
+        wanted, conv_kernel, grads, mixed, raw, key_weight, value_weight
+    )
     grad_states, grad_key_weight, grad_value_weight = spread(
         asked_flat, back, weight_sums, local_blocks
     )

time: 227 us -> 225 us (level)
  Pallas kernels: 217 us -> 201 us
  local copies, waits for them, and re-layouts: 8.74 us -> 21.2 us
    pallas_call x1, Pallas kernels: 52.5 us -> 24 us  [core(): pl.pallas_call(functools.partial(core_kernel, heads), grid=(spans,), in_s...]
    unnamed x8 -> x24, local copies, waits for them, and re-layouts: 7 us -> 19.5 us
    pallas_call x1, Pallas kernels: 89 us -> 101 us  [tail(): pl.pallas_call(functools.partial(tail_kernel, owners, parts), in_specs=[p...]
where the time goes in v4:
time: 225 us; the launch traced here: 224 us
  Pallas kernels  201 us (89%)
  local copies, waits for them, and re-layouts  21.2 us (9%)
    pallas_call x1, Pallas kernels, tail(): pl.pallas_call(functools.partial(tail_kernel, owners, parts), in_specs=[p...  101 us
    pallas_call x1, Pallas kernels, fetch(): pl.pallas_call(functools.partial(fetch_kernel, owners, parts), in_specs=[...  66.1 us
    pallas_call x1, Pallas kernels, core(): pl.pallas_call(functools.partial(core_kernel, heads), grid=(spans,), in_s...  24 us
    unnamed x24, local copies, waits for them, and re-layouts  19.5 us
    pallas_call x1, Pallas kernels, spread(): pl.pallas_call(spread_kernel, grid=(max(heads, CHUNKS),), in_specs=[pl.Bl...  9.72 us

profile of v4, /device:TPU:1, one launch (start us, length us, event | category | flops | bytes accessed | tf_op | source)
XLA Modules:
  0.0 224.1 jit_solution(15410232844234680834)
XLA Ops:
  0.6 0.8 copy.20
  1.4 0.1 reshape.48
  1.5 0.2 convert_reduce_fusion
  1.7 0.1 fusion
  1.8 0.8 copy.21
  2.5 0.1 broadcast_in_dim.29
  2.6 0.6 select_reduce_fusion
  3.2 0.1 select_n.23
  3.4 0.0 copy-start.2
  3.4 1.5 copy-done.2
  4.9 66.1 %shard_map.127 = (bf16[7,4,18,32,128]{4,3,2,1,0:T(8,128)(2,1)S(1)}, s32[32,1,128]{2,1,0:T(1,128)S(1)}) custom-call(s32[18]{0:T(128)S(1)} %multiply_add_fusion.slot_ref, s32[32,1,128]{2,1,0:T(1,128)S(1)} %pad.4.table_ref, bf16[32,32,896]{2,1,0:T(8,128)(2,1)S(1)} %copy-done.2), custom_call_target="tpu_custom_call" | custom-call | bytes 16000000 | tf_op jit(solution)/shard_map/pallas_call | solution.py:288
  71.0 0.0 copy-start.3
  71.0 2.0 copy-done.3
  73.1 0.1 reshape_squeeze.3.rows_ref
  73.2 0.0 copy-start.4
  73.2 2.2 copy-done.4
  75.4 0.0 copy-start.5
  75.4 1.5 copy-done.5
  76.9 0.0 copy-start.6
  76.9 1.5 copy-done.6
  78.4 0.0 copy-start.7
  78.4 1.3 copy-done.7
  79.6 0.0 copy-start.8
  79.6 1.3 copy-done.8
  80.9 0.7 copy-done.9
  81.6 24.0 %shard_map.128 = (bf16[576,1024]{1,0:T(8,128)(2,1)}, bf16[576,1024]{1,0:T(8,128)(2,1)}, bf16[2,2304,1024]{2,1,0:T(8,128)(2,1)}, bf16[896,2304]{1,0:T(8,128)(2,1)S(1)}) custom-call(bf16[576,1024]{1,0:T(8,128)(2,1)S(1)} %copy-done.7, bf16[576,1024]{1,0:T(8,128)(2,1)S(1)} %copy-done.8, bf16[7,4,18,32,128]{4,3,2,1,0:T(8,128)(2,1)S(1)} %copy-done.4, ...), custom_call_target="tpu_custom_call" | custom-call | flops 10000000000 | bytes 30000000 | tf_op jit(solution)/shard_map/pallas_call | solution.py:115
  105.6 1.9 copy-done.10
  107.5 101.4 %shard_map.129 = (bf16[7,64,32,128]{3,2,1,0:T(8,128)(2,1)}, bf16[2,8,4,224,128]{4,3,2,1,0:T(8,128)(2,1)}, f32[8,896]{1,0:T(8,128)}) custom-call(s32[64]{0:T(128)} %get-tuple-element.30.req_ref, f32[3,896]{1,0:T(4,128)} %conv_ref.1, bf16[2,2304,1024]{2,1,0:T(8,128)(2,1)} %get-tuple-element.22.grads_hbm, bf16[896,2304]{1,0:T(8,128)(2,1)} %copy-done.10, ...), custom_call_target="tpu_custom_call" | custom-call | flops 16999999488 | bytes 30000000 | tf_op jit(solution)/shard_map/pallas_call | solution.py:734
  209.0 1.4 slice.7
  210.3 2.0 copy-done
  212.4 2.0 copy-done.1
  214.4 9.7 %shard_map.130 = (f32[32,32,896]{2,1,0:T(8,128)}, f32[896,1024]{1,0:T(8,128)}, f32[896,1024]{1,0:T(8,128)}) custom-call(s32[64]{0:T(128)S(1)} %reshape_squeeze.3.rows_ref, bf16[7,64,32,128]{3,2,1,0:T(8,128)(2,1)S(1)} %copy-done, bf16[2,8,896,128]{3,2,1,0:T(8,128)(2,1)S(1)} %bitcast.2), custom_call_target="tpu_custom_call" | custom-call | bytes 19000000 | tf_op jit(solution)/shard_map/pallas_call | solution.py:813
  (8 shorter events, 0.1 us)
Async XLA Ops:
  3.4 1.5 copy-start.2
  71.0 2.0 copy-start.3
  73.2 2.2 copy-start.4
  75.4 1.5 copy-start.5
  76.9 1.5 copy-start.6
  78.4 1.3 copy-start.7
  79.6 1.3 copy-start.8
  80.9 0.7 copy-start.9
  105.6 1.9 copy-start.10
  210.3 2.0 copy-start
  212.4 2.0 copy-start.1

commit v5 on v4

--- a/solution.py
+++ b/solution.py
@@ -142,7 +142,7 @@
             pltpu.VMEM((heads, 2 * SPAN, keys_here), BF16),
         ],
         compiler_params=pltpu.CompilerParams(
-            dimension_semantics=("arbitrary",), vmem_limit_bytes=40 * 1024 * 1024
+            dimension_semantics=("arbitrary",), vmem_limit_bytes=60 * 1024 * 1024
         ),
         cost_estimate=pl.CostEstimate(
             flops=10_000_000_000, bytes_accessed=30_000_000, transcendentals=1_200_000
@@ -213,7 +213,7 @@
     pltpu.make_async_copy(asked_ref, asked_s, local_sem).start()
     pltpu.make_async_copy(asked_ref, asked_s, local_sem).wait()
 
-    for c in range(CHUNKS):
+    def replies(c):
         cols = slice(c * LANES, (c + 1) * LANES)
 
         def reply(step, carry):
@@ -235,6 +235,10 @@
             row = jnp.maximum(asked_s[me, 0, k], 0)
             recv[c][capacity * me + k] = states_ref[row, :, cols]
 
+    ahead = 2
+    for c in range(ahead):
+        replies(c)
+
     def along_y(kind, c, part, rows, side):
         block = raw_ref.at[c, part, rows]
         return pltpu.make_async_remote_copy(
@@ -253,6 +257,8 @@
         return along_y(kind, c, part, rows, right)
 
     for c in range(CHUNKS + 1):
+        if c + ahead < CHUNKS:
+            replies(c + ahead)
         if c < CHUNKS:
             most = recv[c].at[pl.ds(0, capacity * others)]
             pltpu.make_async_copy(most, most, recv_sem.at[c]).wait()
@@ -305,7 +311,7 @@
         ]
         + [pltpu.VMEM((2 * owners, quarter, LANES), BF16)] * CHUNKS,
         compiler_params=pltpu.CompilerParams(
-            collective_id=0, has_side_effects=True, vmem_limit_bytes=40 * 1024 * 1024
+            collective_id=0, has_side_effects=True, vmem_limit_bytes=60 * 1024 * 1024
         ),
         cost_estimate=pl.CostEstimate(flops=0, bytes_accessed=16_000_000, transcendentals=0),
     )(slots, table, states)
@@ -380,13 +386,10 @@
             grads_hbm.at[:, rows], grads.at[:, rows], grads_sem.at[span]
         )
 
-    load(0).start()
-    load(1).start()
-    load_grads(0).start()
-    load(2).start()
-    for span in range(1, spans):
+    for span in range(spans):
         load_grads(span).start()
-    load(3).start()
+    for index in (3, 0, 1, 2):
+        load(index).start()
     taps_acc[...] = jnp.zeros_like(taps_acc)
     half = requests // 2
     capacity = 2
@@ -415,12 +418,10 @@
             src_ref=src, dst_ref=dst, send_sem=send_sem, recv_sem=recv_sem, device_id=where
         )
 
-    def grad_columns(chunks, first):
+    def grad_columns(chunks):
         cols = slice(chunks[0] * LANES, (chunks[-1] + 1) * LANES)
 
         def one(span, carry):
-            if first:
-                load_grads(span).wait()
             rows = pl.ds(pl.multiple_of(span * keys_here, keys_here), keys_here)
             whole = lax.dot_general(
                 grads[0, rows], kw_ref[cols], NT, preferred_element_type=F32
@@ -443,13 +444,6 @@
 
         lax.fori_loop(0, spans, one, 0)
 
-    def weight_terms(which, pair):
-        wide = pl.ds(pair * 2 * HD, 2 * HD)
-        term = jnp.dot(mixed_t[...], grads[which, :, wide], preferred_element_type=F32)
-        for i in (0, 1):
-            block = term[:, i * HD : (i + 1) * HD].astype(BF16)
-            w_ref[which, 2 * pair + i] = block.reshape(4, -1, HD)
-
     def far_copy(side, c):
         rows, to = ((low, right), (high, left))[side]
         return remote(
@@ -511,14 +505,25 @@
     def group(h, step):
         return h * 4 + lax.rem(first_at[h] + step, 4)
 
-    def pair_copy(g):
+    def pair_copy(d, h):
+        g = group(h, d)
         return remote(
             w_ref.at[1 - core, g],
             sibling_w.at[g],
-            pair_send.at[0, g],
-            pair_recv.at[0, g],
+            pair_send.at[0, h * 4 + d],
+            pair_recv.at[0, h * 4 + d],
             {"dp": sibling},
         )
+
+    def weight_terms(which, d):
+        def columns(h):
+            return grads[which, :, pl.ds(pl.multiple_of(group(h, d) * HD, HD), HD)]
+
+        both = jnp.concatenate([columns(0), columns(1)], axis=1)
+        term = jnp.dot(mixed_t[...], both, preferred_element_type=F32)
+        for h in (0, 1):
+            block = term[:, h * HD : (h + 1) * HD].astype(BF16)
+            w_ref[which, group(h, d)] = block.reshape(4, -1, HD)
 
     def first_copy(d, h):
         return remote(
@@ -569,6 +574,7 @@
         )
 
     def pair_sum(d, h):
+        pair_copy(d, h).wait_recv()
         g = group(h, d)
         pair_w[g] = (w_ref[core, g].astype(F32) + sibling_w[g].astype(F32)).astype(BF16)
         if d:
@@ -639,67 +645,67 @@
             total = total + taps_in[stage, other]
         return total
 
-    load(0).wait()
-    load(1).wait()
-    load(2).wait()
-    grad_columns((0, 1), True)
-    for c in (0, 1):
-        far_copy(0, c).start()
-        far_copy(1, c).start()
+    def start_far(chunks):
+        for c in chunks:
+            far_copy(0, c).start()
+            far_copy(1, c).start()
+
+    for span in range(spans):
+        load_grads(span).wait()
     load(3).wait()
-    for pair in range(4):
-        weight_terms(1 - core, pair)
-        pair_copy(2 * pair).start()
-        pair_copy(2 * pair + 1).start()
-        if pair in (1, 2):
-            forward(pair - 1)
-    for pair in range(4):
-        weight_terms(core, pair)
-        if pair in (1, 3):
-            give_back(pair // 2)
-    for g in range(8):
-        pair_copy(g).wait_recv()
-    for d, h in order:
-        pair_sum(d, h)
-    grad_columns((2, 3), False)
-    for c in (2, 3):
-        far_copy(0, c).start()
-        far_copy(1, c).start()
-    grad_columns((4, 5), False)
-    for c in (4, 5):
-        far_copy(0, c).start()
-        far_copy(1, c).start()
+    steps = (1, 2, 3, 0)
+    for i, d in enumerate(steps):
+        weight_terms(1 - core, d)
+        pair_copy(d, 0).start()
+        pair_copy(d, 1).start()
+        weight_terms(core, d)
+        if i:
+            pair_sum(steps[i - 1], 0)
+            pair_sum(steps[i - 1], 1)
+    pair_sum(steps[-1], 0)
+    pair_sum(steps[-1], 1)
+    for index in (0, 1, 2):
+        load(index).wait()
+    grad_columns((0, 1))
+    start_far((0, 1))
+    sum_first(0)
+    sum_first(1)
+    grad_columns((2, 3))
+    start_far((2, 3))
+    forward(0)
+    forward(1)
+    sum_second(0)
+    sum_second(1)
+    grad_columns((4, 5))
+    start_far((4, 5))
+    give_back(0)
+    gather_first(0)
+    gather_first(1)
     forward(2)
     forward(3)
-    sum_first(0)
-    sum_first(1)
-    grad_columns((6,), False)
-    far_copy(0, 6).start()
-    far_copy(1, 6).start()
+    grad_columns((6,))
+    start_far((6,))
     taps_start(0, jnp.sum(taps_acc[...], axis=1))
-    give_back(2)
+    give_back(1)
     forward(4)
     forward(5)
-    sum_second(0)
-    sum_second(1)
-    give_back(3)
+    give_back(2)
     forward(6)
     taps_start(1, taps_end(0))
-    gather_first(0)
-    gather_first(1)
+    give_back(3)
+    taps_start(2, taps_end(1))
     give_back(4)
-    taps_start(2, taps_end(1))
+    taps_start(3, taps_end(2))
     give_back(5)
-    taps_start(3, taps_end(2))
-    give_back(6)
     gather_pair(0)
     gather_pair(1)
+    give_back(6)
     tsum_ref[...] = taps_end(3)
 
     for d, h in order:
         pair_gather(d, h, 1 - core).wait_recv()
         pair_gather(d, h, core).wait_send()
-        pair_copy(h * 4 + d).wait_send()
+        pair_copy(d, h).wait_send()
         if d:
             first_copy(d, h).wait_send()
             second_copy(d, h).wait_send()
@@ -793,16 +799,18 @@
     def _():
         states_ref[...] = jnp.zeros_like(states_ref)
 
-        def add(slot, carry):
-            row = rows_ref[slot]
-
-            @pl.when(row >= 0)
-            def _():
-                states_ref[row] += back_ref[0, slot].astype(F32)
+        def add(index, carry):
+            for k in range(8):
+                slot = index * 8 + k
+                row = rows_ref[slot]
+
+                @pl.when(row >= 0)
+                def _():
+                    states_ref[row] += back_ref[0, slot].astype(F32)
 
             return carry
 
-        lax.fori_loop(0, rows_ref.shape[0], add, 0)
+        lax.fori_loop(0, rows_ref.shape[0] // 8, add, 0)
 
 
 def spread(rows, back, weights, blocks):
@@ -829,7 +837,7 @@
             jax.ShapeDtypeStruct((ENC, heads * HD), F32),
         ],
         compiler_params=pltpu.CompilerParams(
-            dimension_semantics=("arbitrary",), vmem_limit_bytes=32 * 1024 * 1024
+            dimension_semantics=("arbitrary",), vmem_limit_bytes=60 * 1024 * 1024
         ),
         cost_estimate=pl.CostEstimate(flops=0, bytes_accessed=19_000_000, transcendentals=0),
     )(rows, back, weights.reshape(2, heads, ENC, HD))

time: 225 us -> 216 us (0.960)
  local copies, waits for them, and re-layouts: 21.2 us -> 5.18 us
  Pallas kernels: 201 us -> 208 us
    unnamed x24 -> x4, local copies, waits for them, and re-layouts: 19.5 us -> 1.54 us
    pallas_call x1, Pallas kernels: 66.1 us -> 69.1 us  [fetch(): pl.pallas_call(functools.partial(fetch_kernel, owners, parts), in_specs=[...]
where the time goes in v5:
time: 216 us; the launch traced here: 215 us
  Pallas kernels  208 us (96%)
  local copies, waits for them, and re-layouts  5.18 us (2%)
    pallas_call x1, Pallas kernels, tail(): pl.pallas_call(functools.partial(tail_kernel, owners, parts), in_specs=[p...  102 us
    pallas_call x1, Pallas kernels, fetch(): pl.pallas_call(functools.partial(fetch_kernel, owners, parts), in_specs=[...  69.1 us
    pallas_call x1, Pallas kernels, core(): pl.pallas_call(functools.partial(core_kernel, heads), grid=(spans,), in_s...  26.3 us
    pallas_call x1, Pallas kernels, spread(): pl.pallas_call(spread_kernel, grid=(max(heads, CHUNKS),), in_specs=[pl.Bl...  10.8 us

profile of v5, /device:TPU:1, one launch (start us, length us, event | category | flops | bytes accessed | tf_op | source)
XLA Modules:
  0.0 215.0 jit_solution(12477962422190346715)
XLA Ops:
  0.6 0.8 copy.20
  1.4 0.1 reshape.48
  1.5 0.2 convert_reduce_fusion
  1.7 0.0 copy-start
  1.7 0.1 fusion
  1.8 0.8 copy.21
  2.5 0.1 broadcast_in_dim.29
  2.6 0.6 select_reduce_fusion
  3.2 0.1 select_n.23
  3.3 0.6 pad.4.table_ref
  4.0 0.0 copy-done
  4.0 69.1 %shard_map.127 = (bf16[7,4,18,32,128]{4,3,2,1,0:T(8,128)(2,1)}, s32[32,1,128]{2,1,0:T(1,128)}) custom-call(s32[18]{0:T(128)} %copy-done, s32[32,1,128]{2,1,0:T(1,128)} %pad.4.table_ref, bf16[32,32,896]{2,1,0:T(8,128)(2,1)} %states_ref.1), custom_call_target="tpu_custom_call" | custom-call | bytes 16000000 | tf_op jit(solution)/shard_map/pallas_call | solution.py:294
  73.1 0.8 slice_reduce_fusion
  73.9 0.6 reshape_squeeze.3.rows_ref
  74.5 26.3 %shard_map.128 = (bf16[576,1024]{1,0:T(8,128)(2,1)}, bf16[576,1024]{1,0:T(8,128)(2,1)}, bf16[2,2304,1024]{2,1,0:T(8,128)(2,1)}, bf16[896,2304]{1,0:T(8,128)(2,1)}) custom-call(bf16[576,1024]{1,0:T(8,128)(2,1)} %q_ref.1, bf16[576,1024]{1,0:T(8,128)(2,1)} %g_ref.1, bf16[7,4,18,32,128]{4,3,2,1,0:T(8,128)(2,1)} %get-tuple-element.18.raw_ref.raw_hbm, ...), custom_call_target="tpu_custom_call" | custom-call | flops 10000000000 | bytes 30000000 | tf_op jit(solution)/shard_map/pallas_call | solution.py:115
  100.8 102.0 %shard_map.129 = (bf16[7,64,32,128]{3,2,1,0:T(8,128)(2,1)}, bf16[2,8,4,224,128]{4,3,2,1,0:T(8,128)(2,1)}, f32[8,896]{1,0:T(8,128)}) custom-call(s32[64]{0:T(128)} %get-tuple-element.30.req_ref, f32[3,896]{1,0:T(4,128)} %conv_ref.1, bf16[2,2304,1024]{2,1,0:T(8,128)(2,1)} %get-tuple-element.22.grads_hbm, bf16[896,2304]{1,0:T(8,128)(2,1)} %get-tuple-element.23.mixed_hbm, ...), custom_call_target="tpu_custom_call" | custom-call | flops 16999999488 | bytes 30000000 | tf_op jit(solution)/shard_map/pallas_call | solution.py:740
  202.8 1.4 slice.7
  204.2 10.8 %shard_map.130 = (f32[32,32,896]{2,1,0:T(8,128)}, f32[896,1024]{1,0:T(8,128)}, f32[896,1024]{1,0:T(8,128)}) custom-call(s32[64]{0:T(128)} %reshape_squeeze.3.rows_ref, bf16[7,64,32,128]{3,2,1,0:T(8,128)(2,1)} %get-tuple-element.24.back_ref, bf16[2,8,896,128]{3,2,1,0:T(8,128)(2,1)} %bitcast.2), custom_call_target="tpu_custom_call" | custom-call | bytes 19000000 | tf_op jit(solution)/shard_map/pallas_call | solution.py:821
  (2 shorter events, 0.0 us)
Async XLA Ops:
  1.7 2.3 %copy-start = (s32[18]{0:T(128)}, s32[18]{0:T(128)S(1)}, u32[]{:S(2)}) copy-start(s32[18]{0:T(128)S(1)} %multiply_add_fusion.slot_ref) | copy-start | bytes 220

commit v6 on v5

--- a/solution.py
+++ b/solution.py
@@ -386,10 +386,12 @@
             grads_hbm.at[:, rows], grads.at[:, rows], grads_sem.at[span]
         )
 
+    load(0).start()
+    load(1).start()
     for span in range(spans):
         load_grads(span).start()
-    for index in (3, 0, 1, 2):
-        load(index).start()
+    load(2).start()
+    load(3).start()
     taps_acc[...] = jnp.zeros_like(taps_acc)
     half = requests // 2
     capacity = 2
@@ -650,56 +652,63 @@
             far_copy(0, c).start()
             far_copy(1, c).start()
 
-    for span in range(spans):
-        load_grads(span).wait()
-    load(3).wait()
-    steps = (1, 2, 3, 0)
-    for i, d in enumerate(steps):
+    def weight_step(d):
         weight_terms(1 - core, d)
         pair_copy(d, 0).start()
         pair_copy(d, 1).start()
         weight_terms(core, d)
-        if i:
-            pair_sum(steps[i - 1], 0)
-            pair_sum(steps[i - 1], 1)
-    pair_sum(steps[-1], 0)
-    pair_sum(steps[-1], 1)
+
+    def pair_sums(d):
+        pair_sum(d, 0)
+        pair_sum(d, 1)
+
+    for span in range(spans):
+        load_grads(span).wait()
     for index in (0, 1, 2):
         load(index).wait()
     grad_columns((0, 1))
     start_far((0, 1))
+    load(3).wait()
+    weight_step(1)
+    forward(0)
+    forward(1)
+    weight_step(2)
+    pair_sums(1)
+    give_back(0)
+    weight_step(3)
+    pair_sums(2)
+    give_back(1)
+    weight_step(0)
+    pair_sums(3)
+    pair_sums(0)
+    grad_columns((2, 3))
+    start_far((2, 3))
+    grad_columns((4, 5))
+    start_far((4, 5))
+    forward(2)
+    forward(3)
     sum_first(0)
     sum_first(1)
-    grad_columns((2, 3))
-    start_far((2, 3))
-    forward(0)
-    forward(1)
+    grad_columns((6,))
+    start_far((6,))
+    give_back(2)
+    forward(4)
+    forward(5)
     sum_second(0)
     sum_second(1)
-    grad_columns((4, 5))
-    start_far((4, 5))
-    give_back(0)
+    taps_start(0, jnp.sum(taps_acc[...], axis=1))
+    give_back(3)
+    forward(6)
     gather_first(0)
     gather_first(1)
-    forward(2)
-    forward(3)
-    grad_columns((6,))
-    start_far((6,))
-    taps_start(0, jnp.sum(taps_acc[...], axis=1))
-    give_back(1)
-    forward(4)
-    forward(5)
-    give_back(2)
-    forward(6)
     taps_start(1, taps_end(0))
-    give_back(3)
+    give_back(4)
     taps_start(2, taps_end(1))
-    give_back(4)
+    give_back(5)
     taps_start(3, taps_end(2))
-    give_back(5)
+    give_back(6)
     gather_pair(0)
     gather_pair(1)
-    give_back(6)
     tsum_ref[...] = taps_end(3)
 
     for d, h in order:
@@ -791,29 +800,45 @@
     )(wanted, conv_kernel, grads, mixed, raw, key_weight, value_weight)
 
 
-def spread_kernel(rows_ref, back_ref, w_ref, states_ref, gkw_ref, gvw_ref):
+def spread_kernel(
+    asked_ref, back_ref, w_ref, taps_ref, states_ref, gkw_ref, gvw_ref, gt_ref, used, count
+):
     gkw_ref[...] = w_ref[0, 0].astype(F32)
     gvw_ref[...] = w_ref[1, 0].astype(F32)
-
-    @pl.when(pl.program_id(0) < CHUNKS)
+    step = pl.program_id(0)
+
+    @pl.when(step == 0)
+    def _():
+        gt_ref[...] = taps_ref[0:KW]
+        count[0] = 0
+
+        def note(owner, carry):
+            for k in (0, 1):
+                row = asked_ref[owner, 0, k]
+
+                @pl.when(row >= 0)
+                def _():
+                    at = count[0]
+                    used[0, at] = 2 * owner + k
+                    used[1, at] = row
+                    count[0] = at + 1
+
+            return carry
+
+        lax.fori_loop(0, asked_ref.shape[0], note, 0)
+
+    @pl.when(step < CHUNKS)
     def _():
         states_ref[...] = jnp.zeros_like(states_ref)
 
         def add(index, carry):
-            for k in range(8):
-                slot = index * 8 + k
-                row = rows_ref[slot]
-
-                @pl.when(row >= 0)
-                def _():
-                    states_ref[row] += back_ref[0, slot].astype(F32)
-
+            states_ref[used[1, index]] += back_ref[0, used[0, index]].astype(F32)
             return carry
 
-        lax.fori_loop(0, rows_ref.shape[0] // 8, add, 0)
-
-
-def spread(rows, back, weights, blocks):
+        lax.fori_loop(0, count[0], add, 0)
+
+
+def spread(asked, back, weights, taps, blocks):
     heads = weights.shape[1]
     slots, quarter = back.shape[1], back.shape[2]
     last = CHUNKS - 1
@@ -825,57 +850,82 @@
             pl.BlockSpec(memory_space=pltpu.SMEM),
             pl.BlockSpec((1, slots, quarter, LANES), lambda i: (jnp.minimum(i, last), 0, 0, 0)),
             pl.BlockSpec((2, 1, ENC, HD), lambda i: (0, i, 0, 0)),
+            pl.BlockSpec((8, ENC), lambda i: (0, 0)),
         ],
         out_specs=[
             pl.BlockSpec((blocks, quarter, LANES), lambda i: (0, 0, jnp.minimum(i, last))),
             head_cols,
             head_cols,
+            pl.BlockSpec((KW, ENC), lambda i: (0, 0)),
         ],
         out_shape=[
             jax.ShapeDtypeStruct((blocks, quarter, ENC), F32),
             jax.ShapeDtypeStruct((ENC, heads * HD), F32),
             jax.ShapeDtypeStruct((ENC, heads * HD), F32),
+            jax.ShapeDtypeStruct((KW, ENC), F32),
         ],
+        scratch_shapes=[pltpu.SMEM((2, slots), jnp.int32), pltpu.SMEM((1,), jnp.int32)],
         compiler_params=pltpu.CompilerParams(
             dimension_semantics=("arbitrary",), vmem_limit_bytes=60 * 1024 * 1024
         ),
         cost_estimate=pl.CostEstimate(flops=0, bytes_accessed=19_000_000, transcendentals=0),
-    )(rows, back, weights.reshape(2, heads, ENC, HD))
+    )(asked, back, weights.reshape(2, heads, ENC, HD), taps)
+
+
+def tables_kernel(owner_ref, row_ref, slot_ref, wanted_ref, table_ref, rows, taken):
+    owners = table_ref.shape[0]
+    requests = slot_ref.shape[0]
+
+    def clear(owner, carry):
+        taken[owner] = 0
+        for k in (0, 1):
+            rows[2 * owner + k] = -1
+            wanted_ref[2 * owner + k] = 0
+        return carry
+
+    lax.fori_loop(0, owners, clear, 0)
+    for p in range(requests):
+        owner = owner_ref[p % NBR, p // NBR]
+        slot = 2 * owner + jnp.minimum(taken[owner], 1)
+        taken[owner] = taken[owner] + 1
+        slot_ref[p] = slot
+        rows[slot] = row_ref[p % NBR, p // NBR]
+        wanted_ref[slot] = p
+    lane = lax.broadcasted_iota(jnp.int32, (1, LANES), 1)
+    for owner in range(owners):
+        table_ref[owner] = jnp.where(lane == 0, rows[2 * owner], rows[2 * owner + 1])
+
+
+def tables(nbr_owner, nbr_row, owners):
+    requests = nbr_owner.shape[0] * NBR
+    smem = pl.BlockSpec(memory_space=pltpu.SMEM)
+    return pl.pallas_call(
+        tables_kernel,
+        in_specs=[smem, smem],
+        out_specs=[smem, smem, pl.BlockSpec(memory_space=pltpu.VMEM)],
+        out_shape=[
+            jax.ShapeDtypeStruct((requests,), jnp.int32),
+            jax.ShapeDtypeStruct((2 * owners,), jnp.int32),
+            jax.ShapeDtypeStruct((owners, 1, LANES), jnp.int32),
+        ],
+        scratch_shapes=[pltpu.SMEM((2 * owners,), jnp.int32), pltpu.SMEM((owners,), jnp.int32)],
+        compiler_params=pltpu.CompilerParams(vmem_limit_bytes=60 * 1024 * 1024),
+    )(nbr_owner.T, nbr_row.T)
 
 
 def shards(
     queries, cotangent, db_states, key_weight, value_weight, conv_kernel, nbr_owner, nbr_row
 ):
-    owners = lax.axis_size("dp")
-    span_count = nbr_owner.shape[0]
-    request_count = span_count * NBR
-    capacity = max(2, (request_count + owners - 1) // owners)
-    quarter = db_states.shape[1]
-    local_blocks = db_states.shape[0]
-    slots_total = owners * capacity
-    owner_flat = nbr_owner.reshape(request_count)
-    row_flat = nbr_row.reshape(request_count)
-    positions = jnp.arange(request_count, dtype=jnp.int32)
-    same_owner = owner_flat[:, None] == owner_flat[None, :]
-    earlier = positions[:, None] > positions[None, :]
-    slot_index = jnp.sum(jnp.logical_and(same_owner, earlier).astype(jnp.int32), axis=1)
-    target = owner_flat * capacity + slot_index
-    slot_hits = target[:, None] == jnp.arange(slots_total, dtype=jnp.int32)[None, :]
-    used_slot = jnp.any(slot_hits, axis=0)
-    row_sent = jnp.sum(jnp.where(slot_hits, row_flat[:, None], 0), axis=0)
-    row_table = jnp.where(used_slot, row_sent, -1).reshape(owners, capacity)
-    wanted = jnp.sum(jnp.where(slot_hits, positions[:, None], 0), axis=0)
-    table = jnp.pad(row_table[:, None, :], ((0, 0), (0, 0), (0, LANES - capacity)))
-    raw, asked = fetch(target, table, db_states)
-    asked_flat = asked[:, 0, :capacity].reshape(slots_total)
+    slots, wanted, table = tables(nbr_owner, nbr_row, lax.axis_size("dp"))
+    raw, asked = fetch(slots, table, db_states)
     attended, grad_query, grads, mixed = core(
         queries, cotangent, raw, key_weight, value_weight, conv_kernel
     )
     back, weight_sums, taps_sum = tail(
         wanted, conv_kernel, grads, mixed, raw, key_weight, value_weight
     )
-    grad_states, grad_key_weight, grad_value_weight = spread(
-        asked_flat, back, weight_sums, local_blocks
+    grad_states, grad_key_weight, grad_value_weight, grad_kernel = spread(
+        asked, back, weight_sums, taps_sum, db_states.shape[0]
     )
     return (
         attended,
@@ -883,7 +933,7 @@
         grad_states,
         grad_key_weight,
         grad_value_weight,
-        taps_sum[:KW],
+        grad_kernel,
     )
 
 

time: 216 us -> 212 us (0.981)
  local copies, waits for them, and re-layouts: 5.18 us -> 0 us
where the time goes in v6:
time: 212 us; the launch traced here: 211 us
  Pallas kernels  210 us (99%)
    pallas_call x1, Pallas kernels, tail(): pl.pallas_call(functools.partial(tail_kernel, owners, parts), in_specs=[p...  103 us
    pallas_call x1, Pallas kernels, fetch(): pl.pallas_call(functools.partial(fetch_kernel, owners, parts), in_specs=[...  69.2 us
    pallas_call x1, Pallas kernels, core(): pl.pallas_call(functools.partial(core_kernel, heads), grid=(spans,), in_s...  26.3 us
    pallas_call x1, Pallas kernels, spread(): pl.pallas_call(spread_kernel, grid=(max(heads, CHUNKS),), in_specs=[pl.Bl...  10.1 us

profile of v6, /device:TPU:1, one launch (start us, length us, event | category | flops | bytes accessed | tf_op | source)
XLA Modules:
  0.0 211.1 jit_solution(14859302614499436655)
XLA Ops:
  0.6 1.7 shard_map.127
  2.3 69.2 %shard_map.128 = (bf16[7,4,18,32,128]{4,3,2,1,0:T(8,128)(2,1)}, s32[32,1,128]{2,1,0:T(1,128)}) custom-call(s32[18]{0:T(128)} %get-tuple-element.22.slot_ref, s32[32,1,128]{2,1,0:T(1,128)} %get-tuple-element.23.table_ref, bf16[32,32,896]{2,1,0:T(8,128)(2,1)} %states_ref.1), custom_call_target="tpu_custom_call" | custom-call | bytes 16000000 | tf_op jit(solution)/shard_map/pallas_call | solution.py:294
  71.6 26.3 %shard_map.129 = (bf16[576,1024]{1,0:T(8,128)(2,1)}, bf16[576,1024]{1,0:T(8,128)(2,1)}, bf16[2,2304,1024]{2,1,0:T(8,128)(2,1)}, bf16[896,2304]{1,0:T(8,128)(2,1)}) custom-call(bf16[576,1024]{1,0:T(8,128)(2,1)} %q_ref.1, bf16[576,1024]{1,0:T(8,128)(2,1)} %g_ref.1, bf16[7,4,18,32,128]{4,3,2,1,0:T(8,128)(2,1)} %get-tuple-element.24.raw_ref.raw_hbm, ...), custom_call_target="tpu_custom_call" | custom-call | flops 10000000000 | bytes 30000000 | tf_op jit(solution)/shard_map/pallas_call | solution.py:115
  97.9 103.0 %shard_map.130 = (bf16[7,64,32,128]{3,2,1,0:T(8,128)(2,1)}, bf16[2,8,4,224,128]{4,3,2,1,0:T(8,128)(2,1)}, f32[8,896]{1,0:T(8,128)}) custom-call(s32[64]{0:T(128)} %get-tuple-element.28.req_ref, f32[3,896]{1,0:T(4,128)} %conv_ref.1, bf16[2,2304,1024]{2,1,0:T(8,128)(2,1)} %get-tuple-element.29.grads_hbm, bf16[896,2304]{1,0:T(8,128)(2,1)} %get-tuple-element.30.mixed_hbm, ...), custom_call_target="tpu_custom_call" | custom-call | flops 16999999488 | bytes 30000000 | tf_op jit(solution)/shard_map/pallas_call | solution.py:749
  200.9 10.1 %shard_map.131 = (f32[32,32,896]{2,1,0:T(8,128)}, f32[896,1024]{1,0:T(8,128)}, f32[896,1024]{1,0:T(8,128)}, f32[3,896]{1,0:T(4,128)}) custom-call(s32[32,1,128]{2,1,0:T(1,128)} %get-tuple-element.27.asked_ref, bf16[7,64,32,128]{3,2,1,0:T(8,128)(2,1)} %get-tuple-element.31.back_ref, bf16[2,8,896,128]{3,2,1,0:T(8,128)(2,1)} %bitcast.3, ...), custom_call_target="tpu_custom_call" | custom-call | bytes 19000000 | tf_op jit(solution)/shard_map/pallas_call | solution.py:846

commit v7 on v6

--- a/solution.py
+++ b/solution.py
@@ -536,6 +536,27 @@
             {"dp": first_peer[h](d)},
         )
 
+    def far_half(side, h):
+        at = (0, h * 3 + 1) if side == 0 else (4, h * 3)
+        return remote(
+            pair_w.at[group(h, 2), pl.ds(2 * side, 2)],
+            first_in.at[h, 1, pl.ds(2 * side, 2)],
+            axis_send.at[at],
+            axis_recv.at[at],
+            {"dp": first_peer[h](1 + 2 * side)},
+        )
+
+    def relay(side, h, back):
+        at = (3, h * 3 + 1) if side == 0 else (4, h * 3 + 1)
+        block = wsum_ref.at[core, group(h, back), pl.ds(2 * side, 2)]
+        return remote(
+            block,
+            block,
+            axis_send.at[at],
+            axis_recv.at[at],
+            {"dp": first_peer[h](1 + 2 * side)},
+        )
+
     def second_copy(d, h):
         return remote(
             first_sum.at[h, lax.rem(second_at[h] + d, 4)],
@@ -578,15 +599,26 @@
     def pair_sum(d, h):
         pair_copy(d, h).wait_recv()
         g = group(h, d)
-        pair_w[g] = (w_ref[core, g].astype(F32) + sibling_w[g].astype(F32)).astype(BF16)
-        if d:
+        total = w_ref[core, g].astype(F32) + sibling_w[g].astype(F32)
+        if d in (1, 3):
+            side = d // 2
+            far_half(side, h).wait_recv()
+            added = total[2 * side : 2 * side + 2]
+            added = added + first_in[h, 1, 2 * side : 2 * side + 2].astype(F32)
+            pair_w[g, 2 * side : 2 * side + 2] = added.astype(BF16)
+            pair_w[g, 2 - 2 * side : 4 - 2 * side] = total[2 - 2 * side : 4 - 2 * side].astype(BF16)
             first_copy(d, h).start()
+        else:
+            pair_w[g] = total.astype(BF16)
+            if d:
+                far_half(0, h).start()
+                far_half(1, h).start()
 
     def sum_first(h):
-        for d in (1, 2, 3):
+        for d in (1, 3):
             first_copy(d, h).wait_recv()
         total = pair_w[group(h, 0)].astype(F32)
-        for d in (1, 2, 3):
+        for d in (1, 3):
             total = total + first_in[h, d - 1].astype(F32)
         first_sum[h] = total.astype(BF16)
         for d in (1, 2, 3):
@@ -605,14 +637,20 @@
     def gather_first(h):
         for d in (1, 2, 3):
             second_gather(d, h, 4 - d).wait_recv()
-        for d in (1, 2, 3):
+        for d in (1, 3):
             first_gather(d, h, 0).start()
         pair_gather(0, h, core).start()
 
-    def gather_pair(h):
-        for d in (1, 2, 3):
+    def gather_relay(h):
+        for side, d in ((0, 1), (1, 3)):
             first_gather(d, h, 4 - d).wait_recv()
+            relay(side, h, 4 - d).start()
             pair_gather(d, h, core).start()
+
+    def gather_far(h):
+        relay(0, h, 2).wait_recv()
+        relay(1, h, 2).wait_recv()
+        pair_gather(2, h, core).start()
 
     stages = (
         (2, core, lambda step: {"dp": sibling}),
@@ -669,14 +707,14 @@
     grad_columns((0, 1))
     start_far((0, 1))
     load(3).wait()
-    weight_step(1)
+    weight_step(2)
     forward(0)
     forward(1)
-    weight_step(2)
-    pair_sums(1)
+    weight_step(1)
+    pair_sums(2)
     give_back(0)
     weight_step(3)
-    pair_sums(2)
+    pair_sums(1)
     give_back(1)
     weight_step(0)
     pair_sums(3)
@@ -705,10 +743,12 @@
     give_back(4)
     taps_start(2, taps_end(1))
     give_back(5)
+    gather_relay(0)
+    gather_relay(1)
     taps_start(3, taps_end(2))
     give_back(6)
-    gather_pair(0)
-    gather_pair(1)
+    gather_far(0)
+    gather_far(1)
     tsum_ref[...] = taps_end(3)
 
     for d, h in order:
@@ -716,10 +756,13 @@
         pair_gather(d, h, core).wait_send()
         pair_copy(d, h).wait_send()
         if d:
-            first_copy(d, h).wait_send()
             second_copy(d, h).wait_send()
             second_gather(d, h, 0).wait_send()
+        if d in (1, 3):
+            first_copy(d, h).wait_send()
             first_gather(d, h, 0).wait_send()
+            far_half(d // 2, h).wait_send()
+            relay(d // 2, h, 4 - d).wait_send()
     for stage in range(4):
         for d in range(1, stages[stage][0]):
             taps_copy(stage, d).wait_send()
@@ -785,8 +828,8 @@
             dma((CHUNKS,)),
             dma((2, 8)),
             dma((2, 8)),
-            dma((4, 6)),
-            dma((4, 6)),
+            dma((5, 6)),
+            dma((5, 6)),
             dma((4, 3)),
             dma((4, 3)),
         ]

time: 212 us -> 208 us (0.981)
  Pallas kernels: 210 us -> 207 us
    pallas_call x1, Pallas kernels: 103 us -> 99.9 us  [tail(): pl.pallas_call(functools.partial(tail_kernel, owners, parts), in_specs=[p...]
where the time goes in v7:
time: 208 us
  Pallas kernels  207 us (100%)
    pallas_call x1, Pallas kernels, tail(): pl.pallas_call(functools.partial(tail_kernel, owners, parts), in_specs=[p...  99.9 us
    pallas_call x1, Pallas kernels, fetch(): pl.pallas_call(functools.partial(fetch_kernel, owners, parts), in_specs=[...  69.2 us
    pallas_call x1, Pallas kernels, core(): pl.pallas_call(functools.partial(core_kernel, heads), grid=(spans,), in_s...  26.3 us
    pallas_call x1, Pallas kernels, spread(): pl.pallas_call(spread_kernel, grid=(max(heads, CHUNKS),), in_specs=[pl.Bl...  10.1 us

profile of v7, /device:TPU:1, one launch (start us, length us, event | category | flops | bytes accessed | tf_op | source)
XLA Modules:
  0.0 208.0 jit_solution(14819810061886577378)
XLA Ops:
  0.6 1.7 shard_map.127
  2.3 69.2 %shard_map.128 = (bf16[7,4,18,32,128]{4,3,2,1,0:T(8,128)(2,1)}, s32[32,1,128]{2,1,0:T(1,128)}) custom-call(s32[18]{0:T(128)} %get-tuple-element.22.slot_ref, s32[32,1,128]{2,1,0:T(1,128)} %get-tuple-element.23.table_ref, bf16[32,32,896]{2,1,0:T(8,128)(2,1)} %states_ref.1), custom_call_target="tpu_custom_call" | custom-call | bytes 16000000 | tf_op jit(solution)/shard_map/pallas_call | solution.py:294
  71.6 26.3 %shard_map.129 = (bf16[576,1024]{1,0:T(8,128)(2,1)}, bf16[576,1024]{1,0:T(8,128)(2,1)}, bf16[2,2304,1024]{2,1,0:T(8,128)(2,1)}, bf16[896,2304]{1,0:T(8,128)(2,1)}) custom-call(bf16[576,1024]{1,0:T(8,128)(2,1)} %q_ref.1, bf16[576,1024]{1,0:T(8,128)(2,1)} %g_ref.1, bf16[7,4,18,32,128]{4,3,2,1,0:T(8,128)(2,1)} %get-tuple-element.24.raw_ref.raw_hbm, ...), custom_call_target="tpu_custom_call" | custom-call | flops 10000000000 | bytes 30000000 | tf_op jit(solution)/shard_map/pallas_call | solution.py:115
  97.9 99.9 %shard_map.130 = (bf16[7,64,32,128]{3,2,1,0:T(8,128)(2,1)}, bf16[2,8,4,224,128]{4,3,2,1,0:T(8,128)(2,1)}, f32[8,896]{1,0:T(8,128)}) custom-call(s32[64]{0:T(128)} %get-tuple-element.28.req_ref, f32[3,896]{1,0:T(4,128)} %conv_ref.1, bf16[2,2304,1024]{2,1,0:T(8,128)(2,1)} %get-tuple-element.29.grads_hbm, bf16[896,2304]{1,0:T(8,128)(2,1)} %get-tuple-element.30.mixed_hbm, ...), custom_call_target="tpu_custom_call" | custom-call | flops 16999999488 | bytes 30000000 | tf_op jit(solution)/shard_map/pallas_call | solution.py:792
  197.8 10.1 %shard_map.131 = (f32[32,32,896]{2,1,0:T(8,128)}, f32[896,1024]{1,0:T(8,128)}, f32[896,1024]{1,0:T(8,128)}, f32[3,896]{1,0:T(4,128)}) custom-call(s32[32,1,128]{2,1,0:T(1,128)} %get-tuple-element.27.asked_ref, bf16[7,64,32,128]{3,2,1,0:T(8,128)(2,1)} %get-tuple-element.31.back_ref, bf16[2,8,896,128]{3,2,1,0:T(8,128)(2,1)} %bitcast.3, ...), custom_call_target="tpu_custom_call" | custom-call | bytes 19000000 | tf_op jit(solution)/shard_map/pallas_call | solution.py:889

commit v8 on v7

--- a/solution.py
+++ b/solution.py
@@ -152,9 +152,15 @@
 
 def dp_peer(step):
     me = lax.axis_index("dp")
-    z = lax.rem(me // 8 + step // 8, 4)
-    x = lax.rem(lax.rem(me // 2, 4) + lax.rem(step // 2, 4), 4)
-    return z * 8 + x * 2 + lax.rem(me + step, 2)
+    index = step - 1
+
+    def distance(i):
+        return (2 + 3 * i + 3 * (i * (i - 1) // 2)) % 4
+
+    z = (me // 8 + distance(index % 16 // 4)) % 4
+    x = (me // 2 + distance(index % 4)) % 4
+    core = (me + 1 + index // 16) % 2
+    return z * 8 + x * 2 + core
 
 
 def fetch_kernel(
@@ -235,7 +241,7 @@
             row = jnp.maximum(asked_s[me, 0, k], 0)
             recv[c][capacity * me + k] = states_ref[row, :, cols]
 
-    ahead = 2
+    ahead = 3
     for c in range(ahead):
         replies(c)
 

time: 208 us -> 212 us (1.019)
  Pallas kernels: 207 us -> 211 us
    pallas_call x1, Pallas kernels: 99.9 us -> 104 us  [tail(): pl.pallas_call(functools.partial(tail_kernel, owners, parts), in_specs=[p...]
where the time goes in v8:
time: 212 us; the launch traced here: 211 us
  Pallas kernels  211 us (100%)
    pallas_call x1, Pallas kernels, tail(): pl.pallas_call(functools.partial(tail_kernel, owners, parts), in_specs=[p...  104 us
    pallas_call x1, Pallas kernels, fetch(): pl.pallas_call(functools.partial(fetch_kernel, owners, parts), in_specs=[...  68.2 us
    pallas_call x1, Pallas kernels, core(): pl.pallas_call(functools.partial(core_kernel, heads), grid=(spans,), in_s...  26.3 us
    pallas_call x1, Pallas kernels, spread(): pl.pallas_call(spread_kernel, grid=(max(heads, CHUNKS),), in_specs=[pl.Bl...  10.1 us

profile of v8, /device:TPU:1, one launch (start us, length us, event | category | flops | bytes accessed | tf_op | source)
XLA Modules:
  0.0 211.4 jit_solution(14871578341442734645)
XLA Ops:
  0.6 1.7 shard_map.127
  2.3 68.2 %shard_map.128 = (bf16[7,4,18,32,128]{4,3,2,1,0:T(8,128)(2,1)}, s32[32,1,128]{2,1,0:T(1,128)}) custom-call(s32[18]{0:T(128)} %get-tuple-element.22.slot_ref, s32[32,1,128]{2,1,0:T(1,128)} %get-tuple-element.23.table_ref, bf16[32,32,896]{2,1,0:T(8,128)(2,1)} %states_ref.1), custom_call_target="tpu_custom_call" | custom-call | bytes 16000000 | tf_op jit(solution)/shard_map/pallas_call | solution.py:300
  70.5 26.3 %shard_map.129 = (bf16[576,1024]{1,0:T(8,128)(2,1)}, bf16[576,1024]{1,0:T(8,128)(2,1)}, bf16[2,2304,1024]{2,1,0:T(8,128)(2,1)}, bf16[896,2304]{1,0:T(8,128)(2,1)}) custom-call(bf16[576,1024]{1,0:T(8,128)(2,1)} %q_ref.1, bf16[576,1024]{1,0:T(8,128)(2,1)} %g_ref.1, bf16[7,4,18,32,128]{4,3,2,1,0:T(8,128)(2,1)} %get-tuple-element.24.raw_ref.raw_hbm, ...), custom_call_target="tpu_custom_call" | custom-call | flops 10000000000 | bytes 30000000 | tf_op jit(solution)/shard_map/pallas_call | solution.py:115
  96.8 104.4 %shard_map.130 = (bf16[7,64,32,128]{3,2,1,0:T(8,128)(2,1)}, bf16[2,8,4,224,128]{4,3,2,1,0:T(8,128)(2,1)}, f32[8,896]{1,0:T(8,128)}) custom-call(s32[64]{0:T(128)} %get-tuple-element.28.req_ref, f32[3,896]{1,0:T(4,128)} %conv_ref.1, bf16[2,2304,1024]{2,1,0:T(8,128)(2,1)} %get-tuple-element.29.grads_hbm, bf16[896,2304]{1,0:T(8,128)(2,1)} %get-tuple-element.30.mixed_hbm, ...), custom_call_target="tpu_custom_call" | custom-call | flops 16999999488 | bytes 30000000 | tf_op jit(solution)/shard_map/pallas_call | solution.py:798
  201.2 10.1 %shard_map.131 = (f32[32,32,896]{2,1,0:T(8,128)}, f32[896,1024]{1,0:T(8,128)}, f32[896,1024]{1,0:T(8,128)}, f32[3,896]{1,0:T(4,128)}) custom-call(s32[32,1,128]{2,1,0:T(1,128)} %get-tuple-element.27.asked_ref, bf16[7,64,32,128]{3,2,1,0:T(8,128)(2,1)} %get-tuple-element.31.back_ref, bf16[2,8,896,128]{3,2,1,0:T(8,128)(2,1)} %bitcast.3, ...), custom_call_target="tpu_custom_call" | custom-call | bytes 19000000 | tf_op jit(solution)/shard_map/pallas_call | solution.py:895
